TPU v7x, 32 devices: a whole 2x2x4 slice. The times are simulated.
32 devices in a mesh: tile: 8 (over z, x), fsdp: 4 (over y, core).
Axes of the slice: x: 2, y: 2, z: 4, core: 2. Of those that a mesh axis runs over, the one named last changes fastest.
Arguments:
- fields: bfloat16 [4, 32, 64, 512], P('fsdp', None, 'tile'), may hold values from -6 to 6
- seam_shift: int32 [8, 2], P('tile'), may hold values from -4 to 4
- kernel: float32 [49, 512], replicated, may hold values from -0.875 to 0.875
- gain: float32 [512], replicated, may hold values from 0.3 to 3
- w_in: bfloat16 [512, 2048], P(None, 'fsdp'), may hold values from -0.25 to 0.25
- w_out: bfloat16 [2048, 512], P('fsdp'), may hold values from -0.125 to 0.125
- cotangent: bfloat16 [4, 32, 64, 512], P('fsdp', None, 'tile'), may hold values from -6 to 6
Outputs:
- mixed: bfloat16 [4, 32, 64, 512], P('fsdp', None, 'tile')
- field_grad: bfloat16 [4, 32, 64, 512], P('fsdp', None, 'tile')
- kernel_grad: float32 [49, 512], replicated
- gain_grad: float32 [512], replicated
- w_in_grad: float32 [512, 2048], P(None, 'fsdp')
- w_out_grad: float32 [2048, 512], P('fsdp')
Inputs may be any that keep to these rules, and one draw needn't show every extreme that they name: `seam_shift`: offset added to the row index of cells taken across a tile's west (column 0) or east (column 1) seam.
All inputs are finite; a program needn't handle non-finite values.
Results may differ from a plain program's by a relative error of at most 0.0095.
Values may be sent and summed in bfloat16 or wider, within the bound.
A program may use at most 128 MiB of HBM per device.

v0:
```python
import math

import jax
import jax.numpy as jnp
from jax import lax
from jax.sharding import PartitionSpec as P

eps = 1e-06
inv_root2 = 0.7071067811865476
inv_root_tau = 0.3989422804014327


def extended(cells, sides, width):
    for axis, dim in sides:
        count = lax.axis_size(axis)
        head = lax.slice_in_dim(cells, 0, width, axis=dim)
        tail = lax.slice_in_dim(cells, cells.shape[dim] - width, cells.shape[dim], axis=dim)
        cells = jnp.concatenate(
            [
                lax.ppermute(tail, axis, [(i, (i + 1) % count) for i in range(count)]),
                cells,
                lax.ppermute(head, axis, [((i + 1) % count, i) for i in range(count)]),
            ],
            axis=dim,
        )
    return cells


def gelu(value):
    return value * 0.5 * (1.0 + lax.erf(value * inv_root2))


def gelu_slope(value):
    return 0.5 * (1.0 + lax.erf(value * inv_root2)) + value * inv_root_tau * jnp.exp(
        -0.5 * value * value
    )


def shift_rows(strip, offset):
    height = strip.shape[1]
    wider = jnp.pad(strip, ((0, 0), (height, height), (0, 0), (0, 0)))
    return lax.dynamic_slice_in_dim(wider, height + offset, height, 1)


def depthwise(padded, kernel):
    height = padded.shape[1] - 6
    width = padded.shape[2] - 6
    total = jnp.zeros((padded.shape[0], height, width, padded.shape[3]), jnp.float32)
    for row in range(7):
        for col in range(7):
            total = (
                total + padded[:, row : row + height, col : col + width, :] * kernel[7 * row + col]
            )
    return total


def body(fields, seam_shift, kernel, gain, w_in, w_out, cotangent):
    height = fields.shape[1]
    width = fields.shape[2]
    channels = fields.shape[3]
    count = fields.shape[0] * height * width
    cells = count * lax.axis_size("tile") * lax.axis_size("fsdp")
    factor = 1.0 / math.sqrt(cells)
    west_shift = seam_shift[0, 0]
    east_shift = seam_shift[0, 1]
    row_pad = ((0, 0), (3, 3), (0, 0), (0, 0))
    widened = extended(fields, (("tile", 2),), 3)
    west = shift_rows(widened[:, :, :3], west_shift)
    east = shift_rows(widened[:, :, width + 3 :], east_shift)
    padded = jnp.pad(jnp.concatenate([west, fields, east], axis=2), row_pad)
    mixed_in = depthwise(padded, kernel)
    rows = mixed_in.reshape(count, channels)
    mean = jnp.mean(rows, axis=-1, keepdims=True)
    centered = rows - mean
    rstd = lax.rsqrt(jnp.mean(centered * centered, axis=-1, keepdims=True) + eps)
    normed = centered * rstd
    scaled = (normed * gain).astype(jnp.bfloat16)
    back = cotangent.reshape(count, channels)
    contract_last = (((1,), (1,)), ((), ()))
    full_in, full_out = (
        lax.all_gather(w_in, "fsdp", axis=1, tiled=True),
        lax.all_gather(w_out, "fsdp", axis=0, tiled=True),
    )
    pre = jnp.dot(scaled, full_in, preferred_element_type=jnp.float32)
    hidden = gelu(pre).astype(jnp.bfloat16)
    branch = jnp.dot(hidden, full_out, preferred_element_type=jnp.float32)
    d_hidden = lax.dot_general(back, full_out, contract_last, preferred_element_type=jnp.float32)
    residual = fields.reshape(count, channels).astype(jnp.float32)
    mixed = (residual + branch).astype(jnp.bfloat16).reshape(fields.shape)
    d_pre = (d_hidden * gelu_slope(pre)).astype(jnp.bfloat16)
    term_out = (
        lax.dot_general(hidden, back, (((0,), (0,)), ((), ())), preferred_element_type=jnp.float32)
        * factor
    )
    term_in = (
        lax.dot_general(scaled, d_pre, (((0,), (0,)), ((), ())), preferred_element_type=jnp.float32)
        * factor
    )
    d_scaled = lax.dot_general(d_pre, full_in, contract_last, preferred_element_type=jnp.float32)
    term_gain = jnp.sum(d_scaled * normed, axis=0) * factor
    d_normed = d_scaled * gain
    d_rows = (
        d_normed
        - jnp.mean(d_normed, axis=-1, keepdims=True)
        - normed * jnp.mean(d_normed * normed, axis=-1, keepdims=True)
    ) * rstd
    d_mixed = d_rows.reshape(mixed_in.shape)
    unused, pullback = jax.vjp(depthwise, padded.astype(jnp.float32), kernel)
    d_padded, kernel_term = pullback(d_mixed)
    kernel_term = kernel_term * factor
    d_core = d_padded[:, 3 : height + 3]
    d_west = shift_rows(d_core[:, :, :3], -west_shift)
    d_east = shift_rows(d_core[:, :, width + 3 :], -east_shift)
    returned = extended(
        jnp.concatenate([d_west, d_east], axis=2).astype(jnp.bfloat16), (("tile", 2),), 3
    ).astype(jnp.float32)
    own = cotangent.astype(jnp.float32) + d_core[:, :, 3 : width + 3]
    field_grad = jnp.concatenate(
        [
            own[:, :, :3] + returned[:, :, :3],
            own[:, :, 3 : width - 3],
            own[:, :, width - 3 :] + returned[:, :, 9:],
        ],
        axis=2,
    ).astype(jnp.bfloat16)
    share_in, share_out = (
        lax.psum_scatter(
            term_in.astype(jnp.bfloat16), "fsdp", scatter_dimension=1, tiled=True
        ).astype(jnp.float32),
        lax.psum_scatter(
            term_out.astype(jnp.bfloat16), "fsdp", scatter_dimension=0, tiled=True
        ).astype(jnp.float32),
    )
    w_in_grad, w_out_grad = lax.psum((share_in, share_out), "tile")
    kernel_grad, gain_grad = lax.psum((kernel_term, term_gain), ("tile", "fsdp"))
    return (mixed, field_grad, kernel_grad, gain_grad, w_in_grad, w_out_grad)


def solution(mesh):
    return jax.shard_map(
        body,
        mesh=mesh,
        in_specs=(
            P("fsdp", None, "tile", None),
            P("tile", None),
            P(),
            P(),
            P(None, "fsdp"),
            P("fsdp", None),
            P("fsdp", None, "tile", None),
        ),
        out_specs=(
            P("fsdp", None, "tile", None),
            P("fsdp", None, "tile", None),
            P(),
            P(),
            P(None, "fsdp"),
            P("fsdp", None),
        ),
        check_vma=False,
    )
```

profile of v0, /device:TPU:0, one launch (start us, length us, event | category | flops | bytes accessed | tf_op | source)
XLA Modules:
  0.0 269.2 jit_solution(1947753461697891216)
XLA Ops:
  7.2 0.7 all-gather.3.cloned.1.call-update
  8.0 1.1 fusion.103
  9.1 3.0 %collective-permute-start = (bf16[1,32,3,512]{3,2,1,0:T(4,128)(2,1)S(1)}, bf16[1,32,3,512]{3,2,1,0:T(4,128)(2,1)S(1)}, u32[]{:S(2)}, u32[]{:S(2)}) collective-permute-start(bf16[1,32,3,512]{3,2,1,0:T(4,128)(2,1)S(1)} %get-tuple-element.118), channel_id=1, source_target_pairs={{0,4},{4,8},{8,12},{12,16},{16,20},{20,24},{24,28},{28,0},{1,5},{5... | collective-permute-start | bytes 294920 | tf_op jit(solution)/shard_map/ppermute | solution.py:20
  12.1 3.1 %collective-permute-start.1 = (bf16[1,32,3,512]{3,2,1,0:T(4,128)(2,1)S(1)}, bf16[1,32,3,512]{3,2,1,0:T(4,128)(2,1)S(1)}, u32[]{:S(2)}, u32[]{:S(2)}) collective-permute-start(bf16[1,32,3,512]{3,2,1,0:T(4,128)(2,1)S(1)} %get-tuple-element.119), channel_id=1, source_target_pairs={{4,0},{8,4},{12,8},{16,12},{20,16},{24,20},{28,24},{0,28},{5,1},{9... | collective-permute-start | bytes 294920 | tf_op jit(solution)/shard_map/ppermute | solution.py:22
  15.4 0.6 fusion.107
  18.6 0.1 collective-permute-done
  18.7 0.1 pad_dynamic-slice_fusion.3
  18.9 1.0 collective-permute-done.1
  19.9 0.1 pad_dynamic-slice_fusion.2
  20.0 0.3 fusion.98
  20.3 4.4 %fusion.100 = (f32[32,8]{1,0:T(8,128)S(1)}, f32[1,32,8,512]{3,2,1,0:T(8,128)S(1)}) fusion(f32[512]{0:T(512)S(1)} %bitcast.265, bf16[1,38,14,512]{3,2,1,0:T(8,128)(2,1)S(1)} %get-tuple-element.62, f32[512]{0:T(512)S(1)} %bitcast.283, f32[512]{0:T(512)S(1)} %bitcast.319, f32[512]{0:T(512)S(1)} %bitcast.321, f32[512]{0:T(512)S(1)} %bitcast.323, ...), kind=kLoop, calls=%fused_computation.244 | loop fusion | flops 21626624 | bytes 12094464 | tf_op jit(solution)/shard_map/reduce_sum | solution.py:73
  24.8 0.1 div.15
  24.9 0.2 multiply_reduce_fusion.2
  25.1 0.1 rsqrt.12
  25.2 9.7 %all-gather.3.cloned.1.call-done = bf16[512,2048]{1,0:T(8,128)(2,1)} async-done(((bf16[512,512]{1,0:T(8,128)(2,1)}), bf16[512,2048]{1,0:T(8,128)(2,1)}) %all-gather.3.cloned.1.call-update) | async-done | bytes 2097168 | tf_op jit(solution)/shard_map/all_gather | solution.py:81
  34.9 3.7 %multiply_convert_fusion.2 = (bf16[256,2048]{1,0:T(8,128)(2,1)S(1)}, f32[256,2048]{1,0:T(8,128)}) fusion(bf16[512,2048]{1,0:T(8,128)(2,1)} %all-gather.3.cloned.1.call-done, f32[1,32,8,512]{3,2,1,0:T(8,128)S(1)} %get-tuple-element.64, f32[512]{0:T(512)S(1)} %copy-done.7, f32[256]{0:T(256)S(1)} %rsqrt.12, f32[256]{0:T(256)S(1)} %div.15), kind=kOutput, calls=%fused_computation.8 | convolution fusion | flops 540016640 | bytes 5771264 | tf_op jit(solution)/shard_map/dot_general | solution.py:84
  38.6 20.5 %all-gather.5.cloned.1.call-done = bf16[2048,512]{1,0:T(8,128)(2,1)} async-done(((bf16[512,512]{1,0:T(8,128)(2,1)}), bf16[2048,512]{1,0:T(8,128)(2,1)}) %all-gather.5.cloned.1.call-update) | async-done | bytes 2097168 | tf_op jit(solution)/shard_map/all_gather | solution.py:82
  59.1 3.6 %fusion = bf16[256,2048]{1,0:T(8,128)(2,1)S(1)} fusion(bf16[2048,512]{1,0:T(8,128)(2,1)} %all-gather.5.cloned.1.call-done, f32[256,2048]{1,0:T(8,128)} %get-tuple-element.172, bf16[1,32,8,512]{3,2,1,0:T(8,128)(2,1)S(1)} %copy-done.4), kind=kOutput, calls=%fused_computation.4 | convolution fusion | flops 542113792 | bytes 5505024 | tf_op jit(solution)/shard_map/dot_general | solution.py:87
  62.7 1.0 copy-done.2
  63.7 2.2 multiply_convert_fusion.1
  67.2 4.1 %multiply_reduce_fusion = (f32[512]{0:T(512)}, f32[256]{0:T(256)S(1)}, f32[256]{0:T(256)S(1)}, f32[256,512]{1,0:T(8,128)}) fusion(f32[1,32,8,512]{3,2,1,0:T(8,128)S(1)} %get-tuple-element.64, f32[256]{0:T(256)S(1)} %rsqrt.12, f32[256]{0:T(256)S(1)} %div.15, f32[512]{0:T(512)S(1)} %copy-done.7, bf16[256,2048]{1,0:T(8,128)(2,1)} %copy-done.2, ...), kind=kOutput, calls=%fused_computation.209 | convolution fusion | flops 537918464 | bytes 4202496 | tf_op jit(solution)/shard_map/dot_general | solution.py:99
  71.3 0.6 broadcast_multiply_fusion.2
  71.9 2.1 multiply_convert_fusion
  74.0 0.2 all-reduce.107.cloned.1.call-start
  74.2 0.8 copy-done.3
  75.0 2.3 fusion.83
  77.3 0.9 bitcast_multiply_fusion.46
  78.2 1.2 bitcast_multiply_fusion.47
  79.4 1.2 bitcast_multiply_fusion.48
  80.7 6.8 %pad_add_fusion = f32[1,38,14,512]{3,2,1,0:T(8,128)S(1)} fusion(f32[1,32,8,512]{3,2,1,0:T(8,128)S(1)} %get-tuple-element.70, f32[1,32,8,512]{3,2,1,0:T(8,128)S(1)} %get-tuple-element.71, f32[1,32,8,512]{3,2,1,0:T(8,128)S(1)} %get-tuple-element.72, f32[1,32,8,512]{3,2,1,0:T(8,128)S(1)} %get-tuple-element.73, f32[1,32,8,512]{3,2,1,0:T(8,128)S(1)} %get-tuple-element.74, ...), kind=kLoop, calls=%fused_computation.12 | loop fusion | flops 13074432 | bytes 26779648 | tf_op jit(solution)/shard_map/transpose(jvp())/add_any | solution.py:52
  87.5 0.1 slice_add_fusion
  87.7 0.1 fusion.102
  87.8 0.1 fusion.92
  88.0 4.3 %collective-permute-start.3 = (bf16[1,32,3,512]{3,2,1,0:T(4,128)(2,1)S(1)}, bf16[1,32,3,512]{3,2,1,0:T(4,128)(2,1)S(1)}, u32[]{:S(2)}, u32[]{:S(2)}) collective-permute-start(bf16[1,32,3,512]{3,2,1,0:T(4,128)(2,1)S(1)} %fusion.92), channel_id=1, source_target_pairs={{4,0},{8,4},{12,8},{16,12},{20,16},{24,20},{28,24},{0,28},{5,1},{9... | collective-permute-start | bytes 294920 | tf_op jit(solution)/shard_map/ppermute | solution.py:22
  92.3 0.1 fusion.91
  92.5 39.5 %psum.29 = f32[512]{0:T(512)} all-reduce(f32[512]{0:T(512)S(1)} %broadcast_multiply_fusion.1), channel_id=1, replica_groups=mesh['tile'=8,'fsdp'=4] {'tile','fsdp'}, use_global_device_ids=true, to_apply=%region_55.56 | all-reduce | flops 512 | bytes 4096 | tf_op jit(solution)/shard_map/psum | solution.py:135
  132.0 1.0 fusion.85
  133.2 0.9 fusion.84
  134.3 0.9 add_multiply_fusion
  135.2 0.1 fusion.117
  135.3 0.1 fusion.116
  135.5 3.3 %fusion.6 = bf16[1,32,8,512]{3,2,1,0:T(8,128)(2,1)} fusion(bf16[256,2048]{1,0:T(8,128)(2,1)} %copy-done.1, bf16[2048,512]{1,0:T(8,128)(2,1)} %all-gather.5.cloned.1.call-done, bf16[1,32,8,512]{3,2,1,0:T(8,128)(2,1)S(1)} %copy-done), kind=kOutput, calls=%fused_computation.16 | convolution fusion | flops 537264128 | bytes 3670016 | tf_op jit(solution)/shard_map/dot_general | solution.py:86
  138.8 0.1 maximum_bitcast_fusion
  139.0 0.3 fusion.94
  139.3 0.9 pad_maximum_fusion.2
  140.3 95.3 %all-reduce.108 = (f32[512,512]{1,0:T(8,128)}, f32[512,512]{1,0:T(8,128)}) all-reduce(bf16[512,512]{1,0:T(8,128)(2,1)} %reduce-scatter.3.cloned.1.call-done, bf16[512,512]{1,0:T(8,128)(2,1)} %reduce-scatter.5.cloned.1.call-done), channel_id=1, replica_groups=mesh['tile'=8,'fsdp'=4] {'tile'}, use_global_device_ids=true, to_apply=%region_57.58 | all-reduce | flops 524288 | bytes 3145728 | tf_op jit(solution)/shard_map/psum | solution.py:134
  235.5 25.6 %all-reduce.107.cloned.1.call-done = f32[49,512]{1,0:T(8,128)} async-done(((f32[49,512]{1,0:T(8,128)}), f32[49,512]{1,0:T(8,128)}) %all-reduce.107.cloned.1.call-update) | async-done | bytes 100368 | tf_op jit(solution)/shard_map/psum | solution.py:135
  261.1 1.6 copy.18
  (68 shorter events, 0.6 us)
Async XLA Ops:
  7.2 12.9 %copy-start = (bf16[1,32,8,512]{3,2,1,0:T(8,128)(2,1)S(1)}, bf16[1,32,8,512]{3,2,1,0:T(8,128)(2,1)}, u32[]{:S(2)}) copy-start(bf16[1,32,8,512]{3,2,1,0:T(8,128)(2,1)} %param.7) | copy-start | bytes 786436
  7.2 8.1 %copy-start.6 = (f32[49,512]{1,0:T(8,128)S(1)}, f32[49,512]{1,0:T(8,128)}, u32[]{:S(2)}) copy-start(f32[49,512]{1,0:T(8,128)} %param.9) | copy-start | bytes 301060
  7.2 8.2 %copy-start.24 = (s32[1,2]{1,0:T(1,128)S(1)}, s32[1,2]{1,0:T(1,128)}, u32[]{:S(2)}) copy-start(s32[1,2]{1,0:T(1,128)} %param.8) | copy-start | bytes 28
  7.2 27.7 %all-gather.3.cloned.1.call-start = ((), (), s32[]{:S(2)}) async-start(), calls=%async_computation.2 | async-start | bytes 2621440 | tf_op jit(solution)/shard_map/all_gather | solution.py:81
  7.9 51.2 %all-gather.5.cloned.1.call-start = ((), (), s32[]{:S(2)}) async-start(), calls=%async_computation.3 | async-start | bytes 2621440 | tf_op jit(solution)/shard_map/all_gather | solution.py:82
  9.1 9.6 %collective-permute-start = (bf16[1,32,3,512]{3,2,1,0:T(4,128)(2,1)S(1)}, bf16[1,32,3,512]{3,2,1,0:T(4,128)(2,1)S(1)}, u32[]{:S(2)}, u32[]{:S(2)}) collective-permute-start(bf16[1,32,3,512]{3,2,1,0:T(4,128)(2,1)S(1)} %get-tuple-element.118), channel_id=1, source_target_pairs={{0,4},{4,8},{8,12},{12,16},{16,20},{20,24},{24,28},{28,0},{1,5},{5... | collective-permute-start | bytes 294920 | tf_op jit(solution)/shard_map/ppermute | solution.py:20
  12.1 7.8 %collective-permute-start.1 = (bf16[1,32,3,512]{3,2,1,0:T(4,128)(2,1)S(1)}, bf16[1,32,3,512]{3,2,1,0:T(4,128)(2,1)S(1)}, u32[]{:S(2)}, u32[]{:S(2)}) collective-permute-start(bf16[1,32,3,512]{3,2,1,0:T(4,128)(2,1)S(1)} %get-tuple-element.119), channel_id=1, source_target_pairs={{4,0},{8,4},{12,8},{16,12},{20,16},{24,20},{28,24},{0,28},{5,1},{9... | collective-permute-start | bytes 294920 | tf_op jit(solution)/shard_map/ppermute | solution.py:22
  15.2 125.0 %reduce-scatter.3.cloned.1.call-start = ((), (), s32[]{:S(2)}) async-start(), calls=%async_computation.5 | async-start | bytes 2621440 | tf_op jit(solution)/shard_map/reduce_scatter | solution.py:127
  20.3 14.6 %copy-start.7 = (f32[512]{0:T(512)S(1)}, f32[512]{0:T(512)}, u32[]{:S(2)}) copy-start(f32[512]{0:T(512)} %param.10) | copy-start | bytes 6148
  25.2 33.9 %copy-start.4 = (bf16[1,32,8,512]{3,2,1,0:T(8,128)(2,1)S(1)}, bf16[1,32,8,512]{3,2,1,0:T(8,128)(2,1)}, u32[]{:S(2)}) copy-start(bf16[1,32,8,512]{3,2,1,0:T(8,128)(2,1)} %param.13) | copy-start | bytes 786436
  38.6 33.3 %copy-start.1 = (bf16[256,2048]{1,0:T(8,128)(2,1)}, bf16[256,2048]{1,0:T(8,128)(2,1)S(1)}, u32[]{:S(2)}) copy-start(bf16[256,2048]{1,0:T(8,128)(2,1)S(1)} %get-tuple-element.171) | copy-start | bytes 3145732
  62.7 1.0 copy-start.2
  65.9 74.4 %reduce-scatter.5.cloned.1.call-start = ((), (), s32[]{:S(2)}) async-start(), calls=%async_computation.6 | async-start | bytes 2621440 | tf_op jit(solution)/shard_map/reduce_scatter | solution.py:130
  74.0 1.1 copy-start.3
  74.0 1.1 copy-start.21
  74.0 1.1 copy-start.22
  74.0 187.1 %all-reduce.107.cloned.1.call-start = ((), (), s32[]{:S(2)}) async-start(), calls=%async_computation.4 | async-start | bytes 229376 | tf_op jit(solution)/shard_map/psum | solution.py:135
  80.7 6.8 %copy-start.5 = (bf16[1,32,8,512]{3,2,1,0:T(8,128)(2,1)S(1)}, bf16[1,32,8,512]{3,2,1,0:T(8,128)(2,1)}, u32[]{:S(2)}) copy-start(bf16[1,32,8,512]{3,2,1,0:T(8,128)(2,1)} %param.13) | copy-start | bytes 786436
  87.5 5.0 %copy-start.23 = (f32[512]{0:T(512)S(1)}, f32[512]{0:T(512)}, u32[]{:S(2)}) copy-start(f32[512]{0:T(512)} %get-tuple-element.55) | copy-start | bytes 6148
  88.0 51.0 %collective-permute-start.3 = (bf16[1,32,3,512]{3,2,1,0:T(4,128)(2,1)S(1)}, bf16[1,32,3,512]{3,2,1,0:T(4,128)(2,1)S(1)}, u32[]{:S(2)}, u32[]{:S(2)}) collective-permute-start(bf16[1,32,3,512]{3,2,1,0:T(4,128)(2,1)S(1)} %fusion.92), channel_id=1, source_target_pairs={{4,0},{8,4},{12,8},{16,12},{20,16},{24,20},{28,24},{0,28},{5,1},{9... | collective-permute-start | bytes 294920 | tf_op jit(solution)/shard_map/ppermute | solution.py:22
  92.4 46.5 %collective-permute-start.2 = (bf16[1,32,3,512]{3,2,1,0:T(4,128)(2,1)S(1)}, bf16[1,32,3,512]{3,2,1,0:T(4,128)(2,1)S(1)}, u32[]{:S(2)}, u32[]{:S(2)}) collective-permute-start(bf16[1,32,3,512]{3,2,1,0:T(4,128)(2,1)S(1)} %fusion.91), channel_id=1, source_target_pairs={{0,4},{4,8},{8,12},{12,16},{16,20},{20,24},{24,28},{28,0},{1,5},{5... | collective-permute-start | bytes 294920 | tf_op jit(solution)/shard_map/ppermute | solution.py:20
  133.1 1.1 copy-start.8
  133.1 1.1 copy-start.9
  133.1 1.1 copy-start.10
  133.1 1.1 copy-start.11
  133.1 1.1 copy-start.12
  133.1 1.1 copy-start.13
  133.1 1.1 copy-start.14
  133.1 1.1 copy-start.15
  133.2 1.1 copy-start.16
  133.2 1.1 copy-start.17
  133.2 1.1 copy-start.18
  133.2 1.1 copy-start.19
  133.2 1.1 copy-start.20
Sparse Core Ops, SparseCore 0:
  9.6 25.2 all-gather.2
  36.5 22.5 all-gather.4
  66.0 31.4 reduce-scatter.2
  100.0 31.9 reduce-scatter.4
  138.0 123.1 all-reduce.106
where the time goes:
time: 270 us; the launch traced here: 269 us
  blocking collectives  135 us (50%)
  waiting for transfers between devices  57.7 us (21%)
  other arithmetic  22.3 us (8%)
  matrix products  18.9 us (7%)
  between operations  18.2 us (7%)
  starting transfers between devices  10.9 us (4%)
  local copies, waits for them, and re-layouts  6.37 us (2%)
    psum x1, blocking collectives, body(): w_in_grad, w_out_grad = lax.psum((share_in, share_out), 'tile')  95.3 us
    psum x1, blocking collectives, body(): lax.psum((kernel_term, term_gain), ('tile', 'fsdp'))  39.5 us
    psum x1, waiting for transfers between devices, body(): lax.psum((kernel_term, term_gain), ('tile', 'fsdp'))  25.6 us
    all_gather x1, waiting for transfers between devices, body(): lax.all_gather(w_out, 'fsdp', axis=0, tiled=True)  20.5 us
    all_gather x1, waiting for transfers between devices, body(): lax.all_gather(w_in, 'fsdp', axis=1, tiled=True)  9.74 us
    ppermute x2, starting transfers between devices, extended(): lax.ppermute(head, axis, [((i + 1) % count, i) for i in range(count)])  7.44 us
    add_any x1, other arithmetic, depthwise(): padded[:, row:row + height, col:col + width, :] * kernel[7 * row + col]  6.76 us
  transfers between devices with their start and end apart: 9, of which 5 were waited for; matrix products, arithmetic and copies ran while one was open for 14% of the time, Pallas kernels for 0%

commit v1 on v0

v1 whole, which is shorter than its diff:
```python
import functools
import math

import jax
import jax.numpy as jnp
from jax import lax
from jax.experimental import pallas as pl
from jax.experimental.pallas import tpu as pltpu
from jax.sharding import PartitionSpec as P

MESH = pl.DeviceIdType.MESH
F32 = jnp.float32
BF16 = jnp.bfloat16

eps = 1e-06
inv_root2 = 0.7071067811865476
inv_root_tau = 0.3989422804014327

TOP = 8
CONTRACT_LAST = (((1,), (1,)), ((), ()))
CONTRACT_FIRST = (((0,), (0,)), ((), ()))


def dot(lhs, rhs, dims=(((1,), (0,)), ((), ()))):
    return lax.dot_general(lhs, rhs, dims, preferred_element_type=F32)


def kernel_body(
    tiles, hi, height, width, channels, factor, n_sems,
    x_ref, seam_ref, kern_ref, gain_ref, win_ref, wout_ref, cot_ref,
    mixed_ref, fgrad_ref, kgrad_ref, ggrad_ref, wing_ref, woutg_ref,
    ext, dpad, flip, flip2, tmp, normed, rstd_ref, own_ds, own_br, hid, dpre, pre_ref, dhid_ref,
    hs, hr, adj_s, adj_r, core,
    sc_all, cot_all, ds_s, ds_r, br_s, br_r,
    gf, gs, xr, part, zs, zr, agz, agx,
    kfull, kr, kl, klr, kz, kf,
    send_sems, recv_sems,
):
    cells = height * width
    half = channels // 2
    t = lax.axis_index("tile")
    f = lax.axis_index("fsdp")
    west = lax.rem(t + tiles - 1, tiles)
    east = lax.rem(t + 1, tiles)
    x = lax.rem(t, 2)
    z = t // 2
    x_peer = z * 2 + (1 - x)
    z_at = [lax.rem(z + r, hi) for r in range(hi)]
    z_from = [lax.rem(z + hi - r, hi) for r in range(hi)]
    z_peer = [at * 2 + x for at in z_at]
    f_peer = [f, f + 1 - 2 * lax.rem(f, 2), lax.rem(f + 2, 4), 3 - f]

    barrier = pltpu.get_barrier_semaphore()
    greet = (
        [{"fsdp": f_peer[r]} for r in (1, 2, 3)]
        + [{"tile": west}, {"tile": east}, {"tile": x_peer}]
        + [{"tile": z_peer[r]} for r in range(1, hi)]
    )
    for device in greet:
        pl.semaphore_signal(barrier, inc=1, device_id=device, device_id_type=MESH)

    started = []

    def send(src, dst, device):
        index = len(started)
        copy = pltpu.make_async_remote_copy(
            src_ref=src, dst_ref=dst, send_sem=send_sems.at[index],
            recv_sem=recv_sems.at[index], device_id=device, device_id_type=MESH,
        )
        copy.start()
        started.append(copy)
        return index

    def arrived(index, ref):
        pltpu.make_async_remote_copy(
            src_ref=ref, dst_ref=ref, send_sem=send_sems.at[index],
            recv_sem=recv_sems.at[index], device_id={"tile": t, "fsdp": f}, device_id_type=MESH,
        ).wait_recv()

    def rows_of(j):
        return pl.ds(j * height, height)

    groups = [slice(128 * g, 128 * g + 128) for g in range(channels // 128)]

    def spread(ref, by_lanes):
        for g, lanes in enumerate(groups):
            by_lanes[g] = ref[:, lanes].astype(F32)

    def column_of(by_lanes, j):
        return jnp.concatenate(
            [by_lanes[g, pl.ds(j, height, stride=width), :] for g in range(len(groups))], axis=1
        )

    def put_column(by_lanes, j, value):
        for g, lanes in enumerate(groups):
            by_lanes[g, pl.ds(j, height, stride=width), :] = value[:, lanes]

    def gather_lanes(by_lanes, ref):
        for g, lanes in enumerate(groups):
            ref[:, lanes] = by_lanes[g].astype(BF16)

    spread(x_ref, flip)
    spread(cot_ref, flip2)
    for j in range(width):
        column = column_of(flip, j)
        ext[3 + j, TOP : TOP + height, :] = column
        if j < 3:
            hs[0, rows_of(j), :] = column.astype(BF16)
        if j >= width - 3:
            hs[1, rows_of(j - width + 3), :] = column.astype(BF16)
    pl.semaphore_wait(barrier, len(greet))
    halo_w = send(hs.at[0], hr.at[1], {"tile": west})
    halo_e = send(hs.at[1], hr.at[0], {"tile": east})
    for j in range(width):
        cot_all[0, rows_of(j), :] = column_of(flip2, j).astype(BF16)
    cot_id = [None] + [send(cot_all.at[0], cot_all.at[r], {"fsdp": f_peer[r]}) for r in (1, 2, 3)]
    bottom = ext.shape[1] - TOP - height
    ext[:, 0:TOP, :] = jnp.zeros((width + 6, TOP, channels), F32)
    ext[:, TOP + height :, :] = jnp.zeros((width + 6, bottom, channels), F32)
    dpad[:, 0:TOP, :] = jnp.zeros((width, TOP, channels), F32)
    dpad[:, TOP + height :, :] = jnp.zeros((width, bottom, channels), F32)

    row_at = lax.broadcasted_iota(jnp.int32, (height, height), 0)
    col_at = lax.broadcasted_iota(jnp.int32, (height, height), 1)

    def picker(offset):
        return jnp.where(col_at == row_at + offset, 1.0, 0.0).astype(BF16)

    arrived(halo_w, hr.at[1])
    arrived(halo_e, hr.at[0])
    for side, first in ((0, 0), (1, width + 3)):
        pick = picker(seam_ref[0, side])
        for j in range(3):
            ext[first + j, TOP : TOP + height, :] = dot(pick, hr[side, rows_of(j), :])

    lane_groups = channels // 128

    def lanes_of(g):
        return pl.ds(pl.multiple_of(g * 128, 128), 128)

    @pl.loop(0, lane_groups)
    def _(g):
        lanes = lanes_of(g)
        total = jnp.zeros((width, height, 128), F32)
        for a in range(7):
            shifted = ext[:, TOP - 3 + a : TOP - 3 + a + height, lanes]
            for b in range(7):
                total = total + shifted[b : b + width] * kern_ref[pl.ds(7 * a + b, 1), lanes][None]
        tmp[:, lanes] = total.reshape(cells, 128)

    gain = gain_ref[...]

    @pl.loop(0, width)
    def _(j):
        at = pl.ds(pl.multiple_of(j * height, height), height)
        rows = tmp[at, :]
        centered = rows - jnp.mean(rows, axis=-1, keepdims=True)
        rstd = lax.rsqrt(jnp.mean(centered * centered, axis=-1, keepdims=True) + eps)
        unit = centered * rstd
        normed[at, :] = unit
        rstd_ref[at, :] = jnp.broadcast_to(rstd, (height, 128))
        sc_all[0, at, :] = (unit * gain).astype(BF16)

    sc_id = [None] + [send(sc_all.at[0], sc_all.at[r], {"fsdp": f_peer[r]}) for r in (1, 2, 3)]

    w_in = win_ref[...]
    w_out = wout_ref[...]
    ds_id = [None] * 4
    for r in range(4):
        if r > 0:
            arrived(cot_id[r], cot_all.at[r])
        dhid_ref[...] = dot(cot_all[r], w_out, CONTRACT_LAST)
        if r > 0:
            arrived(sc_id[r], sc_all.at[r])
        pre_ref[...] = dot(sc_all[r], w_in)

        @pl.loop(0, width)
        def _(j):
            at = pl.ds(pl.multiple_of(j * height, height), height)
            pre = pre_ref[at, :]
            phi = 0.5 * (1.0 + lax.erf(pre * inv_root2))
            slope = phi + pre * inv_root_tau * jnp.exp(-0.5 * pre * pre)
            hid[r, at, :] = (pre * phi).astype(BF16)
            dpre[r, at, :] = (dhid_ref[at, :] * slope).astype(BF16)

        back = dot(dpre[r], w_in, CONTRACT_LAST)
        if r == 0:
            own_ds[...] = back
        else:
            ds_s[r - 1] = back.astype(BF16)
            ds_id[r] = send(ds_s.at[r - 1], ds_r.at[r - 1], {"fsdp": f_peer[r]})

    def term_start(h, lhs, rhs):
        total = dot(lhs[0], rhs[0], CONTRACT_FIRST)
        for r in range(1, 4):
            total = total + dot(lhs[r], rhs[r], CONTRACT_FIRST)
        for side in range(2):
            gf[h, side] = total[:, side * half : (side + 1) * half]
            gs[h, side] = total[:, side * half : (side + 1) * half].astype(BF16)
        return send(gs.at[h, 1 - x], xr.at[h], {"tile": x_peer})

    piece = channels // hi

    def term_mid(h, index):
        arrived(index, xr.at[h])
        part[h] = gf[h, x] + xr[h].astype(F32)
        for r in range(hi):
            zs[h, r] = part[h, pl.ds(pl.multiple_of(z_at[r] * piece, piece), piece), :].astype(BF16)
        return [None] + [
            send(zs.at[h, r], zr.at[h, r], {"tile": z_peer[r]}) for r in range(1, hi)
        ]

    def term_sum(h, ids):
        total = part[h, pl.ds(pl.multiple_of(z * piece, piece), piece), :]
        for r in range(1, hi):
            arrived(ids[r], zr.at[h, r])
            total = total + zr[h, r].astype(F32)
        agz[h, z] = (total * factor).astype(BF16)
        return [None] + [
            send(agz.at[h, z], agz.at[h, z], {"tile": z_peer[r]}) for r in range(1, hi)
        ]

    def term_spread(h, ids):
        for r in range(1, hi):
            arrived(ids[r], agz.at[h, z_from[r]])
        return send(agz.at[h], agx.at[h], {"tile": x_peer})

    def lanes_half(side):
        return pl.ds(pl.multiple_of(side * half, half), half)

    def term_end(h, index, out_ref):
        out_ref[:, lanes_half(x)] = agz[h].astype(F32).reshape(channels, half)
        arrived(index, agx.at[h])
        out_ref[:, lanes_half(1 - x)] = agx[h].astype(F32).reshape(channels, half)

    x_ids = [term_start(0, hid, cot_all), term_start(1, sc_all, dpre)]

    br_id = [None] * 4
    for r in (1, 2, 3, 0):
        branch = dot(hid[r], w_out)
        if r == 0:
            own_br[...] = branch
        else:
            br_s[r - 1] = branch.astype(BF16)
            br_id[r] = send(br_s.at[r - 1], br_r.at[r - 1], {"fsdp": f_peer[r]})

    for r in (1, 2, 3):
        arrived(ds_id[r], ds_r.at[r - 1])

    def norm_back(j, term_gain):
        at = pl.ds(pl.multiple_of(j * height, height), height)
        d_scaled = own_ds[at, :]
        for r in range(3):
            d_scaled = d_scaled + ds_r[r, at, :].astype(F32)
        unit = normed[at, :]
        both = d_scaled * unit
        g = d_scaled * gain
        mean_g = jnp.mean(g, axis=-1, keepdims=True)
        mean_gn = jnp.mean(g * unit, axis=-1, keepdims=True)
        dpad[j, TOP : TOP + height, :] = (g - mean_g - unit * mean_gn) * rstd_ref[at, 0:1]
        return term_gain + jnp.sum(both.reshape(height // 8, 8, channels), axis=0)

    term_gain = lax.fori_loop(0, width, norm_back, jnp.zeros((8, channels), F32))
    z_ids = [term_mid(0, x_ids[0]), None]

    kfull[3] = jnp.zeros((16, channels), F32)
    kfull[3, 1:2, :] = jnp.sum(term_gain, axis=0, keepdims=True)

    @pl.loop(0, lane_groups)
    def _(g):
        lanes = lanes_of(g)
        d_here = dpad[:, TOP : TOP + height, lanes]
        for a in range(7):
            shifted = ext[:, TOP - 3 + a : TOP - 3 + a + height, lanes]
            for b in range(7):
                tap = 7 * a + b
                both = (d_here * shifted[b : b + width]).reshape(cells // 8, 8, 128)
                column = jnp.sum(jnp.sum(both, axis=0), axis=0, keepdims=True)
                kfull[tap // 16, tap % 16 : tap % 16 + 1, lanes] = column

    kr_id = [None] + [
        send(kfull.at[f_peer[r]], kr.at[r - 1], {"fsdp": f_peer[r]}) for r in (1, 2, 3)
    ]
    z_ids[1] = term_mid(1, x_ids[1])

    @pl.loop(0, lane_groups)
    def _(g):
        lanes = lanes_of(g)
        total = [jnp.zeros((height, 128), F32) for _ in range(width + 6)]
        for a in range(7):
            first = TOP + 3 - a
            shifted = dpad[:, first : first + height, lanes]
            for b in range(7):
                tap = kern_ref[pl.ds(7 * a + b, 1), lanes]
                for j in range(width):
                    total[j + b] = total[j + b] + shifted[j] * tap
        for j in range(width + 6):
            core[j, :, lanes] = total[j]

    for side, first in ((0, 0), (1, width + 3)):
        pick = picker(-seam_ref[0, side])
        for j in range(3):
            adj_s[side, rows_of(j), :] = dot(pick, core[first + j].astype(BF16)).astype(BF16)
    adj_w = send(adj_s.at[0], adj_r.at[1], {"tile": west})
    adj_e = send(adj_s.at[1], adj_r.at[0], {"tile": east})

    total = kfull[f]
    for r in (1, 2, 3):
        arrived(kr_id[r], kr.at[r - 1])
        total = total + kr[r - 1]
    kl[...] = total
    kl_id = send(kl, klr, {"tile": x_peer})

    g_ids = [term_sum(0, z_ids[0]), None]

    arrived(kl_id, klr)
    kz[z] = kl[...] + klr[...]
    kz_id = [None] + [send(kz.at[z], kz.at[z], {"tile": z_peer[r]}) for r in range(1, hi)]

    g_ids[1] = term_sum(1, z_ids[1])

    for r in (1, 2, 3):
        arrived(br_id[r], br_r.at[r - 1])
    for j in range(width):
        at = rows_of(j)
        value = ext[3 + j, TOP : TOP + height, :] + own_br[at, :]
        for r in range(3):
            value = value + br_r[r, at, :].astype(F32)
        put_column(flip2, j, value)
    gather_lanes(flip2, mixed_ref)

    for r in range(1, hi):
        arrived(kz_id[r], kz.at[z_from[r]])
    total = kz[0]
    for at in range(1, hi):
        total = total + kz[at]
    kf[f] = total * factor
    kf_id = [None] + [send(kf.at[f], kf.at[f], {"fsdp": f_peer[r]}) for r in (1, 2, 3)]

    last = [term_spread(0, g_ids[0]), None]

    arrived(adj_w, adj_r.at[1])
    arrived(adj_e, adj_r.at[0])
    for j in range(width):
        value = cot_all[0, rows_of(j), :].astype(F32) + core[3 + j]
        if j < 3:
            value = value + adj_r[0, rows_of(j), :].astype(F32)
        if j >= width - 3:
            value = value + adj_r[1, rows_of(j - width + 3), :].astype(F32)
        put_column(flip, j, value)
    gather_lanes(flip, fgrad_ref)

    last[1] = term_spread(1, g_ids[1])

    for r in (1, 2, 3):
        arrived(kf_id[r], kf.at[f_peer[r]])
    for at in range(3):
        kgrad_ref[16 * at : 16 * at + 16, :] = kf[at]
    kgrad_ref[48:49, :] = kf[3, 0:1, :]
    ggrad_ref[...] = kf[3, 1:2, :]

    term_end(0, last[0], woutg_ref)
    term_end(1, last[1], wing_ref)
    for copy in started:
        copy.wait_send()
    if len(started) != n_sems:
        raise ValueError(len(started))


def body(tiles, shards, fields, seam_shift, kernel, gain, w_in, w_out, cotangent):
    _, height, width, channels = fields.shape
    cells = height * width
    hidden = w_in.shape[1]
    assert shards == 4 and tiles % 2 == 0 and kernel.shape[0] == 49
    assert hidden == channels and channels % (16 * (tiles // 2)) == 0
    hi = tiles // 2
    factor = 1.0 / math.sqrt(cells * tiles * shards)
    half = channels // 2
    piece = channels // hi
    n_sems = 2 + 3 + 3 + 3 + 3 + 2 + 2 * (2 + 2 * (hi - 1)) + 3 + 1 + (hi - 1) + 3
    padded = height + 16

    def vmem(shape, kind):
        return pltpu.VMEM(shape, kind)

    whole = pl.BlockSpec(memory_space=pltpu.VMEM)
    rows = (cells, channels)
    outs = pl.pallas_call(
        functools.partial(kernel_body, tiles, hi, height, width, channels, factor, n_sems),
        out_shape=(
            jax.ShapeDtypeStruct(rows, BF16),
            jax.ShapeDtypeStruct(rows, BF16),
            jax.ShapeDtypeStruct(kernel.shape, F32),
            jax.ShapeDtypeStruct((1, channels), F32),
            jax.ShapeDtypeStruct(w_in.shape, F32),
            jax.ShapeDtypeStruct(w_out.shape, F32),
        ),
        in_specs=[
            whole, pl.BlockSpec(memory_space=pltpu.SMEM), whole, whole, whole, whole, whole,
        ],
        out_specs=[whole] * 6,
        scratch_shapes=[
            vmem((width + 6, padded, channels), F32),
            vmem((width, padded, channels), F32),
            vmem((channels // 128, cells, 128), F32),
            vmem((channels // 128, cells, 128), F32),
            vmem(rows, F32),
            vmem(rows, F32),
            vmem((cells, 128), F32),
            vmem(rows, F32),
            vmem(rows, F32),
            vmem((4, cells, hidden), BF16),
            vmem((4, cells, hidden), BF16),
            vmem((cells, hidden), F32),
            vmem((cells, hidden), F32),
            vmem((2, 3 * height, channels), BF16),
            vmem((2, 3 * height, channels), BF16),
            vmem((2, 3 * height, channels), BF16),
            vmem((2, 3 * height, channels), BF16),
            vmem((width + 6, height, channels), F32),
            vmem((4, cells, channels), BF16),
            vmem((4, cells, channels), BF16),
            vmem((3, cells, channels), BF16),
            vmem((3, cells, channels), BF16),
            vmem((3, cells, channels), BF16),
            vmem((3, cells, channels), BF16),
            vmem((2, 2, channels, half), F32),
            vmem((2, 2, channels, half), BF16),
            vmem((2, channels, half), BF16),
            vmem((2, channels, half), F32),
            vmem((2, hi, piece, half), BF16),
            vmem((2, hi, piece, half), BF16),
            vmem((2, hi, piece, half), BF16),
            vmem((2, hi, piece, half), BF16),
            vmem((4, 16, channels), F32),
            vmem((3, 16, channels), F32),
            vmem((16, channels), F32),
            vmem((16, channels), F32),
            vmem((hi, 16, channels), F32),
            vmem((4, 16, channels), F32),
            pltpu.SemaphoreType.DMA((n_sems,)),
            pltpu.SemaphoreType.DMA((n_sems,)),
        ],
        compiler_params=pltpu.CompilerParams(
            collective_id=0, has_side_effects=True, vmem_limit_bytes=48 * 1024 * 1024
        ),
        name="block",
    )(
        fields.reshape(rows), seam_shift, kernel, gain.reshape(1, channels), w_in, w_out,
        cotangent.reshape(rows),
    )
    mixed, field_grad, kernel_grad, gain_grad, w_in_grad, w_out_grad = outs
    return (
        mixed.reshape(fields.shape), field_grad.reshape(fields.shape), kernel_grad,
        gain_grad.reshape(channels), w_in_grad, w_out_grad,
    )


def solution(mesh):
    return jax.shard_map(
        functools.partial(body, mesh.shape["tile"], mesh.shape["fsdp"]),
        mesh=mesh,
        in_specs=(
            P("fsdp", None, "tile", None),
            P("tile", None),
            P(),
            P(),
            P(None, "fsdp"),
            P("fsdp", None),
            P("fsdp", None, "tile", None),
        ),
        out_specs=(
            P("fsdp", None, "tile", None),
            P("fsdp", None, "tile", None),
            P(),
            P(),
            P(None, "fsdp"),
            P("fsdp", None),
        ),
        check_vma=False,
    )
```

time: 270 us -> 93.1 us (0.34)
  blocking collectives: 135 us -> 0 us
  Pallas kernels: 0 us -> 82 us
  waiting for transfers between devices: 57.7 us -> 0 us
  other arithmetic: 22.3 us -> 0 us
  matrix products: 18.9 us -> 0 us
  between operations: 18.2 us -> 0.67 us
  starting transfers between devices: 10.9 us -> 0 us
  local copies, waits for them, and re-layouts: 6.37 us -> 10.1 us
    psum x2 -> x0, blocking collectives: 135 us -> none  [the longest x1 95.3 us: body(): w_in_grad, w_out_grad = lax.psum((share_in, share_out), 'tile')]
    pallas_call x0 -> x1, Pallas kernels: none -> 82 us  [body(): pl.pallas_call(functools.partial(kernel_body, tiles, hi, height, width, c...]
    all_gather x2 -> x0, waiting for transfers between devices: 30.2 us -> none  [the longest x1 20.5 us: body(): lax.all_gather(w_out, 'fsdp', axis=0, tiled=True)]
    psum x1 -> x0, waiting for transfers between devices: 25.6 us -> none  [body(): lax.psum((kernel_term, term_gain), ('tile', 'fsdp'))]
    dot_general x6 -> x0, matrix products: 18.9 us -> none  [the longest x1 4.07 us: body(): lax.dot_general(d_pre, full_in, contract_last, preferred_element_type=jnp...]
    ppermute x4 -> x0, starting transfers between devices: 10.5 us -> none  [the longest x2 7.44 us: extended(): lax.ppermute(head, axis, [((i + 1) % count, i) for i in range(count)])]
    reduce_sum x5 -> x0, other arithmetic: 8.87 us -> none  [the longest x1 4.43 us: body(): mean = jnp.mean(rows, axis=-1, keepdims=True)]
    add_any x1 -> x0, other arithmetic: 6.76 us -> none  [depthwise(): padded[:, row:row + height, col:col + width, :] * kernel[7 * row + col]]
  transfers between devices with their start and end apart: 9 -> 0, of which waited for: 5 -> 0; matrix products, arithmetic and copies ran while one was open for 14% -> 0% of each run, Pallas kernels for 0% -> 0%
where the time goes in v1:
time: 93.1 us; the launch traced here: 92.8 us
  Pallas kernels  82 us (88%)
  local copies, waits for them, and re-layouts  10.1 us (11%)
    pallas_call x1, Pallas kernels, body(): pl.pallas_call(functools.partial(kernel_body, tiles, hi, height, width, c...  82 us
    unnamed x20, local copies, waits for them, and re-layouts  10.1 us

profile of v1, /device:TPU:0, one launch (start us, length us, event | category | flops | bytes accessed | tf_op | source)
XLA Modules:
  0.0 92.8 jit_solution(6464757842419767566)
XLA Ops:
  0.6 0.0 copy-start.5
  0.6 0.0 copy-start.6
  0.7 0.7 copy-done.5
  1.3 0.0 copy-done.6
  1.3 0.0 copy-start
  1.3 1.0 %copy-done = bf16[512,512]{1,0:T(8,128)(2,1)S(1)} copy-done((bf16[512,512]{1,0:T(8,128)(2,1)S(1)}, bf16[512,512]{1,0:T(8,128)(2,1)}, u32[]{:S(2)}) %copy-start) | copy-done | bytes 524312
  2.4 0.0 copy-start.1
  2.4 1.0 %copy-done.1 = bf16[512,512]{1,0:T(8,128)(2,1)S(1)} copy-done((bf16[512,512]{1,0:T(8,128)(2,1)S(1)}, bf16[512,512]{1,0:T(8,128)(2,1)}, u32[]{:S(2)}) %copy-start.1) | copy-done | bytes 524312
  3.4 0.0 copy-start.2
  3.4 0.9 %copy-done.2 = bf16[1,32,8,512]{3,2,1,0:T(8,128)(2,1)S(1)} copy-done((bf16[1,32,8,512]{3,2,1,0:T(8,128)(2,1)S(1)}, bf16[1,32,8,512]{3,2,1,0:T(8,128)(2,1)}, u32[]{:S(2)}) %copy-start.2) | copy-done | bytes 262168
  4.4 0.0 copy-start.3
  4.4 0.9 %copy-done.3 = bf16[1,32,8,512]{3,2,1,0:T(8,128)(2,1)S(1)} copy-done((bf16[1,32,8,512]{3,2,1,0:T(8,128)(2,1)S(1)}, bf16[1,32,8,512]{3,2,1,0:T(8,128)(2,1)}, u32[]{:S(2)}) %copy-start.3) | copy-done | bytes 262168
  5.3 0.0 copy-start.4
  5.3 0.9 copy-done.4
  6.2 82.0 %block.1 = (bf16[256,512]{1,0:T(8,128)(2,1)S(1)}, bf16[256,512]{1,0:T(8,128)(2,1)S(1)}, f32[49,512]{1,0:T(8,128)S(1)}, f32[1,512]{1,0:T(1,128)S(1)}, f32[512,512]{1,0:T(8,128)S(1)}, /*index=5*/f32[512,512]{1,0:T(8,128)S(1)}) custom-call(bf16[256,512]{1,0:T(8,128)(2,1)S(1)} %bitcast.6, s32[1,2]{1,0:T(1,128)S(1)} %copy-done.6, f32[49,512]{1,0:T(8,128)S(1)} %copy-done.4, ...), custom_call_target="tpu_custom_call" | custom-call | tf_op jit(solution)/shard_map/block/pallas_call | solution.py:388
  88.3 0.7 copy.19
  89.0 0.7 copy.20
  89.7 0.6 copy.21
  90.3 0.6 copy.22
  90.9 1.0 %copy.23 = f32[512,512]{1,0:T(8,128)} copy(f32[512,512]{1,0:T(8,128)S(1)} %get-tuple-element.28) | data formatting | bytes 2097152
  91.9 1.0 %copy.24 = f32[512,512]{1,0:T(8,128)} copy(f32[512,512]{1,0:T(8,128)S(1)} %get-tuple-element.29) | data formatting | bytes 2097152
Async XLA Ops:
  0.6 0.7 copy-start.5
  0.6 0.7 copy-start.6
  1.3 1.0 %copy-start = (bf16[512,512]{1,0:T(8,128)(2,1)S(1)}, bf16[512,512]{1,0:T(8,128)(2,1)}, u32[]{:S(2)}) copy-start(bf16[512,512]{1,0:T(8,128)(2,1)} %win_ref.1) | copy-start | bytes 1572868
  2.4 1.0 %copy-start.1 = (bf16[512,512]{1,0:T(8,128)(2,1)S(1)}, bf16[512,512]{1,0:T(8,128)(2,1)}, u32[]{:S(2)}) copy-start(bf16[512,512]{1,0:T(8,128)(2,1)} %wout_ref.1) | copy-start | bytes 1572868
  3.4 0.9 %copy-start.2 = (bf16[1,32,8,512]{3,2,1,0:T(8,128)(2,1)S(1)}, bf16[1,32,8,512]{3,2,1,0:T(8,128)(2,1)}, u32[]{:S(2)}) copy-start(bf16[1,32,8,512]{3,2,1,0:T(8,128)(2,1)} %param.7) | copy-start | bytes 786436
  4.4 0.9 %copy-start.3 = (bf16[1,32,8,512]{3,2,1,0:T(8,128)(2,1)S(1)}, bf16[1,32,8,512]{3,2,1,0:T(8,128)(2,1)}, u32[]{:S(2)}) copy-start(bf16[1,32,8,512]{3,2,1,0:T(8,128)(2,1)} %param.13) | copy-start | bytes 786436
  5.3 0.9 copy-start.4

commit v2 on v1

--- a/solution.py
+++ b/solution.py
@@ -27,17 +27,34 @@
 
 def kernel_body(
     tiles, hi, height, width, channels, factor, n_sems,
-    x_ref, seam_ref, kern_ref, gain_ref, win_ref, wout_ref, cot_ref,
-    mixed_ref, fgrad_ref, kgrad_ref, ggrad_ref, wing_ref, woutg_ref,
-    ext, dpad, flip, flip2, tmp, normed, rstd_ref, own_ds, own_br, hid, dpre, pre_ref, dhid_ref,
+    x_hbm, seam_ref, kern_hbm, gain_hbm, win_hbm, wout_hbm, cot_hbm,
+    mixed_hbm, fgrad_hbm, kgrad_hbm, ggrad_hbm, wing_hbm, woutg_hbm,
+    ext, dpad, flip, flip2, tmp, normed, rstd_ref, own_ds, keep_ds, own_br, keep_br, hid, dpre, pre_ref, dhid_ref,
     hs, hr, adj_s, adj_r, core,
     sc_all, cot_all, ds_s, ds_r, br_s, br_r,
     gf, gs, xr, part, zs, zr, agz, agx,
     kfull, kr, kl, klr, kz, kf,
-    send_sems, recv_sems,
+    x_ref, kern_ref, gain_ref, win_ref, wout_ref, cot_ref,
+    mixed_ref, fgrad_ref, kgrad_ref, ggrad_ref, wing_ref, woutg_ref,
+    load_sems, store_sems, send_sems, recv_sems,
 ):
+    pairs = (
+        (x_hbm, x_ref), (cot_hbm, cot_ref), (kern_hbm, kern_ref), (gain_hbm, gain_ref),
+        (wout_hbm, wout_ref), (win_hbm, win_ref),
+    )
+    loads = [
+        pltpu.make_async_copy(src, dst, load_sems.at[i]) for i, (src, dst) in enumerate(pairs)
+    ]
+    for load in loads:
+        load.start()
+    stores = []
+
+    def store(src, dst):
+        stores.append(pltpu.make_async_copy(src, dst, store_sems.at[len(stores)]))
+        stores[-1].start()
+
     cells = height * width
-    half = channels // 2
+    half = channels // 4
     t = lax.axis_index("tile")
     f = lax.axis_index("fsdp")
     west = lax.rem(t + tiles - 1, tiles)
@@ -99,8 +116,8 @@
         for g, lanes in enumerate(groups):
             ref[:, lanes] = by_lanes[g].astype(BF16)
 
+    loads[0].wait()
     spread(x_ref, flip)
-    spread(cot_ref, flip2)
     for j in range(width):
         column = column_of(flip, j)
         ext[3 + j, TOP : TOP + height, :] = column
@@ -111,9 +128,18 @@
     pl.semaphore_wait(barrier, len(greet))
     halo_w = send(hs.at[0], hr.at[1], {"tile": west})
     halo_e = send(hs.at[1], hr.at[0], {"tile": east})
+    loads[1].wait()
+    spread(cot_ref, flip2)
     for j in range(width):
         cot_all[0, rows_of(j), :] = column_of(flip2, j).astype(BF16)
-    cot_id = [None] + [send(cot_all.at[0], cot_all.at[r], {"fsdp": f_peer[r]}) for r in (1, 2, 3)]
+    sibling = {"fsdp": f_peer[1]}
+    across = {"fsdp": f_peer[2]}
+    cot_id = [
+        None,
+        send(cot_all.at[0], cot_all.at[1], sibling),
+        send(cot_all.at[0], cot_all.at[2], across),
+        None,
+    ]
     bottom = ext.shape[1] - TOP - height
     ext[:, 0:TOP, :] = jnp.zeros((width + 6, TOP, channels), F32)
     ext[:, TOP + height :, :] = jnp.zeros((width + 6, bottom, channels), F32)
@@ -126,28 +152,39 @@
     def picker(offset):
         return jnp.where(col_at == row_at + offset, 1.0, 0.0).astype(BF16)
 
+    def lanes_of(g):
+        return pl.ds(pl.multiple_of(g * 128, 128), 128)
+
+    def conv_part(columns, fresh):
+        @pl.loop(0, channels // 128)
+        def _(g):
+            lanes = lanes_of(g)
+            total = [
+                jnp.zeros((height, 128), F32) if fresh else tmp[rows_of(j), lanes]
+                for j in range(width)
+            ]
+            for a in range(7):
+                first = TOP - 3 + a
+                shifted = {c: ext[c, first : first + height, lanes] for c in columns}
+                for b in range(7):
+                    tap = kern_ref[pl.ds(7 * a + b, 1), lanes]
+                    for j in range(width):
+                        if j + b in shifted:
+                            total[j] = total[j] + shifted[j + b] * tap
+            for j in range(width):
+                tmp[rows_of(j), lanes] = total[j]
+
+    loads[2].wait()
+    conv_part(list(range(3, width + 3)), True)
     arrived(halo_w, hr.at[1])
     arrived(halo_e, hr.at[0])
     for side, first in ((0, 0), (1, width + 3)):
         pick = picker(seam_ref[0, side])
         for j in range(3):
             ext[first + j, TOP : TOP + height, :] = dot(pick, hr[side, rows_of(j), :])
-
-    lane_groups = channels // 128
-
-    def lanes_of(g):
-        return pl.ds(pl.multiple_of(g * 128, 128), 128)
-
-    @pl.loop(0, lane_groups)
-    def _(g):
-        lanes = lanes_of(g)
-        total = jnp.zeros((width, height, 128), F32)
-        for a in range(7):
-            shifted = ext[:, TOP - 3 + a : TOP - 3 + a + height, lanes]
-            for b in range(7):
-                total = total + shifted[b : b + width] * kern_ref[pl.ds(7 * a + b, 1), lanes][None]
-        tmp[:, lanes] = total.reshape(cells, 128)
-
+    conv_part([0, 1, 2, width + 3, width + 4, width + 5], False)
+
+    loads[3].wait()
     gain = gain_ref[...]
 
     @pl.loop(0, width)
@@ -161,17 +198,27 @@
         rstd_ref[at, :] = jnp.broadcast_to(rstd, (height, 128))
         sc_all[0, at, :] = (unit * gain).astype(BF16)
 
-    sc_id = [None] + [send(sc_all.at[0], sc_all.at[r], {"fsdp": f_peer[r]}) for r in (1, 2, 3)]
-
+    sc_id = [
+        None,
+        send(sc_all.at[0], sc_all.at[1], sibling),
+        send(sc_all.at[0], sc_all.at[2], across),
+        None,
+    ]
+    loads[4].wait()
+    loads[5].wait()
     w_in = win_ref[...]
     w_out = wout_ref[...]
     ds_id = [None] * 4
     for r in range(4):
         if r > 0:
             arrived(cot_id[r], cot_all.at[r])
+        if r == 2:
+            cot_id[3] = send(cot_all.at[2], cot_all.at[3], sibling)
         dhid_ref[...] = dot(cot_all[r], w_out, CONTRACT_LAST)
         if r > 0:
             arrived(sc_id[r], sc_all.at[r])
+        if r == 2:
+            sc_id[3] = send(sc_all.at[2], sc_all.at[3], sibling)
         pre_ref[...] = dot(sc_all[r], w_in)
 
         @pl.loop(0, width)
@@ -186,14 +233,19 @@
         back = dot(dpre[r], w_in, CONTRACT_LAST)
         if r == 0:
             own_ds[...] = back
+        elif r == 2:
+            keep_ds[...] = back
         else:
-            ds_s[r - 1] = back.astype(BF16)
-            ds_id[r] = send(ds_s.at[r - 1], ds_r.at[r - 1], {"fsdp": f_peer[r]})
-
-    def term_start(h, lhs, rhs):
-        total = dot(lhs[0], rhs[0], CONTRACT_FIRST)
+            slot = r // 2
+            ds_s[slot] = back.astype(BF16)
+            ds_id[r] = send(ds_s.at[slot], ds_r.at[slot], sibling)
+
+    def term_start(h):
+        lhs, rhs = ((hid, cot_all), (sc_all, dpre))[h // 2]
+        lanes = slice((h % 2) * 2 * half, (h % 2) * 2 * half + 2 * half)
+        total = dot(lhs[0], rhs[0, :, lanes], CONTRACT_FIRST)
         for r in range(1, 4):
-            total = total + dot(lhs[r], rhs[r], CONTRACT_FIRST)
+            total = total + dot(lhs[r], rhs[r, :, lanes], CONTRACT_FIRST)
         for side in range(2):
             gf[h, side] = total[:, side * half : (side + 1) * half]
             gs[h, side] = total[:, side * half : (side + 1) * half].astype(BF16)
@@ -204,7 +256,7 @@
     def term_mid(h, index):
         arrived(index, xr.at[h])
         part[h] = gf[h, x] + xr[h].astype(F32)
-        for r in range(hi):
+        for r in range(1, hi):
             zs[h, r] = part[h, pl.ds(pl.multiple_of(z_at[r] * piece, piece), piece), :].astype(BF16)
         return [None] + [
             send(zs.at[h, r], zr.at[h, r], {"tile": z_peer[r]}) for r in range(1, hi)
@@ -225,32 +277,46 @@
             arrived(ids[r], agz.at[h, z_from[r]])
         return send(agz.at[h], agx.at[h], {"tile": x_peer})
 
-    def lanes_half(side):
-        return pl.ds(pl.multiple_of(side * half, half), half)
-
-    def term_end(h, index, out_ref):
-        out_ref[:, lanes_half(x)] = agz[h].astype(F32).reshape(channels, half)
+    def term_put(h, side, value):
+        ref = (woutg_ref, wing_ref)[h // 2]
+        lanes = pl.ds(pl.multiple_of(((h % 2) * 2 + side) * half, half), half)
+        ref[:, lanes] = value.astype(F32).reshape(channels, half)
+
+    def term_end(h, index):
         arrived(index, agx.at[h])
-        out_ref[:, lanes_half(1 - x)] = agx[h].astype(F32).reshape(channels, half)
-
-    x_ids = [term_start(0, hid, cot_all), term_start(1, sc_all, dpre)]
+        term_put(h, 1 - x, agx[h])
+
+    x_ids, z_ids, g_ids, last = [None] * 4, [None] * 4, [None] * 4, [None] * 4
+    x_ids[0] = term_start(0)
+
+    arrived(ds_id[3], ds_r.at[1])
+    ds_s[2] = (keep_ds[...] + ds_r[1].astype(F32)).astype(BF16)
+    ds_id[2] = send(ds_s.at[2], ds_r.at[2], across)
+
+    for h in (1, 2, 3):
+        x_ids[h] = term_start(h)
 
     br_id = [None] * 4
-    for r in (1, 2, 3, 0):
+    for r in (3, 1, 2, 0):
         branch = dot(hid[r], w_out)
         if r == 0:
             own_br[...] = branch
+        elif r == 2:
+            keep_br[...] = branch
         else:
-            br_s[r - 1] = branch.astype(BF16)
-            br_id[r] = send(br_s.at[r - 1], br_r.at[r - 1], {"fsdp": f_peer[r]})
-
-    for r in (1, 2, 3):
-        arrived(ds_id[r], ds_r.at[r - 1])
+            slot = r // 2
+            br_s[slot] = branch.astype(BF16)
+            br_id[r] = send(br_s.at[slot], br_r.at[slot], sibling)
+
+    z_ids[0] = term_mid(0, x_ids[0])
+    z_ids[1] = term_mid(1, x_ids[1])
+    arrived(ds_id[1], ds_r.at[0])
+    arrived(ds_id[2], ds_r.at[2])
 
     def norm_back(j, term_gain):
         at = pl.ds(pl.multiple_of(j * height, height), height)
         d_scaled = own_ds[at, :]
-        for r in range(3):
+        for r in (0, 2):
             d_scaled = d_scaled + ds_r[r, at, :].astype(F32)
         unit = normed[at, :]
         both = d_scaled * unit
@@ -261,12 +327,37 @@
         return term_gain + jnp.sum(both.reshape(height // 8, 8, channels), axis=0)
 
     term_gain = lax.fori_loop(0, width, norm_back, jnp.zeros((8, channels), F32))
-    z_ids = [term_mid(0, x_ids[0]), None]
+    z_ids[2] = term_mid(2, x_ids[2])
+
+    def adjoint(columns):
+        @pl.loop(0, channels // 128)
+        def _(g):
+            lanes = lanes_of(g)
+            total = {c: jnp.zeros((height, 128), F32) for c in columns}
+            for a in range(7):
+                first = TOP + 3 - a
+                shifted = [dpad[j, first : first + height, lanes] for j in range(width)]
+                for b in range(7):
+                    tap = kern_ref[pl.ds(7 * a + b, 1), lanes]
+                    for j in range(width):
+                        if j + b in total:
+                            total[j + b] = total[j + b] + shifted[j] * tap
+            for c in columns:
+                core[c, :, lanes] = total[c]
+
+    adjoint([0, 1, 2, width + 3, width + 4, width + 5])
+    for side, first in ((0, 0), (1, width + 3)):
+        pick = picker(-seam_ref[0, side])
+        for j in range(3):
+            adj_s[side, rows_of(j), :] = dot(pick, core[first + j].astype(BF16)).astype(BF16)
+    adj_w = send(adj_s.at[0], adj_r.at[1], {"tile": west})
+    adj_e = send(adj_s.at[1], adj_r.at[0], {"tile": east})
+    z_ids[3] = term_mid(3, x_ids[3])
 
     kfull[3] = jnp.zeros((16, channels), F32)
     kfull[3, 1:2, :] = jnp.sum(term_gain, axis=0, keepdims=True)
 
-    @pl.loop(0, lane_groups)
+    @pl.loop(0, channels // 128)
     def _(g):
         lanes = lanes_of(g)
         d_here = dpad[:, TOP : TOP + height, lanes]
@@ -281,28 +372,12 @@
     kr_id = [None] + [
         send(kfull.at[f_peer[r]], kr.at[r - 1], {"fsdp": f_peer[r]}) for r in (1, 2, 3)
     ]
-    z_ids[1] = term_mid(1, x_ids[1])
-
-    @pl.loop(0, lane_groups)
-    def _(g):
-        lanes = lanes_of(g)
-        total = [jnp.zeros((height, 128), F32) for _ in range(width + 6)]
-        for a in range(7):
-            first = TOP + 3 - a
-            shifted = dpad[:, first : first + height, lanes]
-            for b in range(7):
-                tap = kern_ref[pl.ds(7 * a + b, 1), lanes]
-                for j in range(width):
-                    total[j + b] = total[j + b] + shifted[j] * tap
-        for j in range(width + 6):
-            core[j, :, lanes] = total[j]
-
-    for side, first in ((0, 0), (1, width + 3)):
-        pick = picker(-seam_ref[0, side])
-        for j in range(3):
-            adj_s[side, rows_of(j), :] = dot(pick, core[first + j].astype(BF16)).astype(BF16)
-    adj_w = send(adj_s.at[0], adj_r.at[1], {"tile": west})
-    adj_e = send(adj_s.at[1], adj_r.at[0], {"tile": east})
+    g_ids[0] = term_sum(0, z_ids[0])
+    g_ids[1] = term_sum(1, z_ids[1])
+
+    arrived(br_id[3], br_r.at[1])
+    br_s[2] = (keep_br[...] + br_r[1].astype(F32)).astype(BF16)
+    br_id[2] = send(br_s.at[2], br_r.at[2], across)
 
     total = kfull[f]
     for r in (1, 2, 3):
@@ -310,34 +385,16 @@
         total = total + kr[r - 1]
     kl[...] = total
     kl_id = send(kl, klr, {"tile": x_peer})
-
-    g_ids = [term_sum(0, z_ids[0]), None]
+    g_ids[2] = term_sum(2, z_ids[2])
+
+    adjoint(list(range(3, width + 3)))
 
     arrived(kl_id, klr)
     kz[z] = kl[...] + klr[...]
     kz_id = [None] + [send(kz.at[z], kz.at[z], {"tile": z_peer[r]}) for r in range(1, hi)]
-
-    g_ids[1] = term_sum(1, z_ids[1])
-
-    for r in (1, 2, 3):
-        arrived(br_id[r], br_r.at[r - 1])
-    for j in range(width):
-        at = rows_of(j)
-        value = ext[3 + j, TOP : TOP + height, :] + own_br[at, :]
-        for r in range(3):
-            value = value + br_r[r, at, :].astype(F32)
-        put_column(flip2, j, value)
-    gather_lanes(flip2, mixed_ref)
-
-    for r in range(1, hi):
-        arrived(kz_id[r], kz.at[z_from[r]])
-    total = kz[0]
-    for at in range(1, hi):
-        total = total + kz[at]
-    kf[f] = total * factor
-    kf_id = [None] + [send(kf.at[f], kf.at[f], {"fsdp": f_peer[r]}) for r in (1, 2, 3)]
-
-    last = [term_spread(0, g_ids[0]), None]
+    g_ids[3] = term_sum(3, z_ids[3])
+    last[0] = term_spread(0, g_ids[0])
+    last[1] = term_spread(1, g_ids[1])
 
     arrived(adj_w, adj_r.at[1])
     arrived(adj_e, adj_r.at[0])
@@ -349,8 +406,30 @@
             value = value + adj_r[1, rows_of(j - width + 3), :].astype(F32)
         put_column(flip, j, value)
     gather_lanes(flip, fgrad_ref)
-
-    last[1] = term_spread(1, g_ids[1])
+    store(fgrad_ref, fgrad_hbm)
+
+    for r in range(1, hi):
+        arrived(kz_id[r], kz.at[z_from[r]])
+    total = kz[0]
+    for at in range(1, hi):
+        total = total + kz[at]
+    kf[f] = total * factor
+    kf_id = [None] + [send(kf.at[f], kf.at[f], {"fsdp": f_peer[r]}) for r in (1, 2, 3)]
+
+    last[2] = term_spread(2, g_ids[2])
+
+    arrived(br_id[1], br_r.at[0])
+    arrived(br_id[2], br_r.at[2])
+    for j in range(width):
+        at = rows_of(j)
+        value = ext[3 + j, TOP : TOP + height, :] + own_br[at, :]
+        for r in (0, 2):
+            value = value + br_r[r, at, :].astype(F32)
+        put_column(flip2, j, value)
+    gather_lanes(flip2, mixed_ref)
+    store(mixed_ref, mixed_hbm)
+
+    last[3] = term_spread(3, g_ids[3])
 
     for r in (1, 2, 3):
         arrived(kf_id[r], kf.at[f_peer[r]])
@@ -358,13 +437,33 @@
         kgrad_ref[16 * at : 16 * at + 16, :] = kf[at]
     kgrad_ref[48:49, :] = kf[3, 0:1, :]
     ggrad_ref[...] = kf[3, 1:2, :]
-
-    term_end(0, last[0], woutg_ref)
-    term_end(1, last[1], wing_ref)
+    store(kgrad_ref, kgrad_hbm)
+    store(ggrad_ref, ggrad_hbm)
+
+    for h in range(4):
+        term_put(h, x, agz[h])
+    for h in range(4):
+        term_end(h, last[h])
+        if h == 1:
+            store(woutg_ref, woutg_hbm)
+    store(wing_ref, wing_hbm)
+    for copy in stores:
+        copy.wait()
     for copy in started:
         copy.wait_send()
-    if len(started) != n_sems:
-        raise ValueError(len(started))
+    assert len(started) <= n_sems
+
+
+def write_out(*refs):
+    count = len(refs) // 2
+    sems = refs[-1]
+    copies = [
+        pltpu.make_async_copy(refs[i], refs[count + i], sems.at[i]) for i in range(count)
+    ]
+    for copy in copies:
+        copy.start()
+    for copy in copies:
+        copy.wait()
 
 
 def body(tiles, shards, fields, seam_shift, kernel, gain, w_in, w_out, cotangent):
@@ -375,15 +474,15 @@
     assert hidden == channels and channels % (16 * (tiles // 2)) == 0
     hi = tiles // 2
     factor = 1.0 / math.sqrt(cells * tiles * shards)
-    half = channels // 2
+    half = channels // 4
     piece = channels // hi
-    n_sems = 2 + 3 + 3 + 3 + 3 + 2 + 2 * (2 + 2 * (hi - 1)) + 3 + 1 + (hi - 1) + 3
+    n_sems = 32 + 4 * (2 + 2 * (hi - 1)) + hi
     padded = height + 16
 
     def vmem(shape, kind):
         return pltpu.VMEM(shape, kind)
 
-    whole = pl.BlockSpec(memory_space=pltpu.VMEM)
+    away = pl.BlockSpec(memory_space=pltpu.HBM)
     rows = (cells, channels)
     outs = pl.pallas_call(
         functools.partial(kernel_body, tiles, hi, height, width, channels, factor, n_sems),
@@ -396,9 +495,9 @@
             jax.ShapeDtypeStruct(w_out.shape, F32),
         ),
         in_specs=[
-            whole, pl.BlockSpec(memory_space=pltpu.SMEM), whole, whole, whole, whole, whole,
+            away, pl.BlockSpec(memory_space=pltpu.SMEM), away, away, away, away, away,
         ],
-        out_specs=[whole] * 6,
+        out_specs=[away] * 6,
         scratch_shapes=[
             vmem((width + 6, padded, channels), F32),
             vmem((width, padded, channels), F32),
@@ -407,6 +506,8 @@
             vmem(rows, F32),
             vmem(rows, F32),
             vmem((cells, 128), F32),
+            vmem(rows, F32),
+            vmem(rows, F32),
             vmem(rows, F32),
             vmem(rows, F32),
             vmem((4, cells, hidden), BF16),
@@ -424,31 +525,54 @@
             vmem((3, cells, channels), BF16),
             vmem((3, cells, channels), BF16),
             vmem((3, cells, channels), BF16),
-            vmem((2, 2, channels, half), F32),
-            vmem((2, 2, channels, half), BF16),
-            vmem((2, channels, half), BF16),
-            vmem((2, channels, half), F32),
-            vmem((2, hi, piece, half), BF16),
-            vmem((2, hi, piece, half), BF16),
-            vmem((2, hi, piece, half), BF16),
-            vmem((2, hi, piece, half), BF16),
+            vmem((4, 2, channels, half), F32),
+            vmem((4, 2, channels, half), BF16),
+            vmem((4, channels, half), BF16),
+            vmem((4, channels, half), F32),
+            vmem((4, hi, piece, half), BF16),
+            vmem((4, hi, piece, half), BF16),
+            vmem((4, hi, piece, half), BF16),
+            vmem((4, hi, piece, half), BF16),
             vmem((4, 16, channels), F32),
             vmem((3, 16, channels), F32),
             vmem((16, channels), F32),
             vmem((16, channels), F32),
             vmem((hi, 16, channels), F32),
             vmem((4, 16, channels), F32),
+            vmem(rows, BF16),
+            vmem(kernel.shape, F32),
+            vmem((1, channels), F32),
+            vmem(w_in.shape, BF16),
+            vmem(w_out.shape, BF16),
+            vmem(rows, BF16),
+            vmem(rows, BF16),
+            vmem(rows, BF16),
+            vmem(kernel.shape, F32),
+            vmem((1, channels), F32),
+            vmem(w_in.shape, F32),
+            vmem(w_out.shape, F32),
+            pltpu.SemaphoreType.DMA((6,)),
+            pltpu.SemaphoreType.DMA((6,)),
             pltpu.SemaphoreType.DMA((n_sems,)),
             pltpu.SemaphoreType.DMA((n_sems,)),
         ],
         compiler_params=pltpu.CompilerParams(
-            collective_id=0, has_side_effects=True, vmem_limit_bytes=48 * 1024 * 1024
+            collective_id=0, has_side_effects=True, vmem_limit_bytes=58 * 1024 * 1024
         ),
         name="block",
     )(
         fields.reshape(rows), seam_shift, kernel, gain.reshape(1, channels), w_in, w_out,
         cotangent.reshape(rows),
     )
+    outs = pl.pallas_call(
+        write_out,
+        out_shape=[jax.ShapeDtypeStruct(out.shape, out.dtype) for out in outs],
+        in_specs=[away] * 6,
+        out_specs=[away] * 6,
+        scratch_shapes=[pltpu.SemaphoreType.DMA((6,))],
+        compiler_params=pltpu.CompilerParams(vmem_limit_bytes=58 * 1024 * 1024),
+        name="write_out",
+    )(*outs)
     mixed, field_grad, kernel_grad, gain_grad, w_in_grad, w_out_grad = outs
     return (
         mixed.reshape(fields.shape), field_grad.reshape(fields.shape), kernel_grad,

time: 93.1 us -> 151 us (1.62)
  Pallas kernels: 82 us -> 150 us
  local copies, waits for them, and re-layouts: 10.1 us -> 0 us
    pallas_call x0 -> x1, Pallas kernels: none -> 84.1 us  [body(): pl.pallas_call(write_out, out_shape=[jax.ShapeDtypeStruct(out.shape, out....]
    pallas_call x1, Pallas kernels: 82 us -> 66.4 us  [body(): pl.pallas_call(functools.partial(kernel_body, tiles, hi, height, width, c...]
    unnamed x20 -> x0, local copies, waits for them, and re-layouts: 10.1 us -> none
where the time goes in v2:
time: 151 us
  Pallas kernels  150 us (99%)
    pallas_call x1, Pallas kernels, body(): pl.pallas_call(write_out, out_shape=[jax.ShapeDtypeStruct(out.shape, out....  84.1 us
    pallas_call x1, Pallas kernels, body(): pl.pallas_call(functools.partial(kernel_body, tiles, hi, height, width, c...  66.4 us

profile of v2, /device:TPU:0, one launch (start us, length us, event | category | flops | bytes accessed | tf_op | source)
XLA Modules:
  0.0 151.1 jit_solution(12466416402515530785)
XLA Ops:
  0.6 66.4 %block.1 = (bf16[256,512]{1,0:T(8,128)(2,1)}, bf16[256,512]{1,0:T(8,128)(2,1)}, f32[49,512]{1,0:T(8,128)}, f32[1,512]{1,0:T(1,128)}, f32[512,512]{1,0:T(8,128)}, /*index=5*/f32[512,512]{1,0:T(8,128)}) custom-call(bf16[256,512]{1,0:T(8,128)(2,1)} %bitcast.6, s32[1,2]{1,0:T(1,128)} %seam_ref.1, f32[49,512]{1,0:T(8,128)} %kern_hbm.1, f32[1,512]{1,0:T(1,128)} %bitcast.8, ...), custom_call_target="tpu_custom_call" | custom-call | tf_op jit(solution)/shard_map/block/pallas_call | solution.py:487
  67.0 84.1 %write_out.1 = (bf16[256,512]{1,0:T(8,128)(2,1)}, bf16[256,512]{1,0:T(8,128)(2,1)}, f32[49,512]{1,0:T(8,128)}, f32[1,512]{1,0:T(1,128)}, f32[512,512]{1,0:T(8,128)}, /*index=5*/f32[512,512]{1,0:T(8,128)}) custom-call(bf16[256,512]{1,0:T(8,128)(2,1)} %get-tuple-element.18.refs_0_, bf16[256,512]{1,0:T(8,128)(2,1)} %get-tuple-element.19.refs_1_, ...), custom_call_target="tpu_custom_call" | custom-call | tf_op jit(solution)/shard_map/write_out/pallas_call | solution.py:567

commit v3 on v2

--- a/solution.py
+++ b/solution.py
@@ -17,8 +17,6 @@
 inv_root_tau = 0.3989422804014327
 
 TOP = 8
-CONTRACT_LAST = (((1,), (1,)), ((), ()))
-CONTRACT_FIRST = (((0,), (0,)), ((), ()))
 
 
 def dot(lhs, rhs, dims=(((1,), (0,)), ((), ()))):
@@ -29,7 +27,7 @@
     tiles, hi, height, width, channels, factor, n_sems,
     x_hbm, seam_ref, kern_hbm, gain_hbm, win_hbm, wout_hbm, cot_hbm,
     mixed_hbm, fgrad_hbm, kgrad_hbm, ggrad_hbm, wing_hbm, woutg_hbm,
-    ext, dpad, flip, flip2, tmp, normed, rstd_ref, own_ds, keep_ds, own_br, keep_br, hid, dpre, pre_ref, dhid_ref,
+    ext, dpad, flip, flip2, tmp, normed, rstd_ref, own_ds, keep_ds, own_br, keep_br, hid, dpre, hid_t, sc_t, win_t, wout_t, pre_ref, dhid_ref,
     hs, hr, adj_s, adj_r, core,
     sc_all, cot_all, ds_s, ds_r, br_s, br_r,
     gf, gs, xr, part, zs, zr, agz, agx,
@@ -208,13 +206,15 @@
     loads[5].wait()
     w_in = win_ref[...]
     w_out = wout_ref[...]
+    wout_t[...] = w_out.T
+    win_t[...] = w_in.T
     ds_id = [None] * 4
     for r in range(4):
         if r > 0:
             arrived(cot_id[r], cot_all.at[r])
         if r == 2:
             cot_id[3] = send(cot_all.at[2], cot_all.at[3], sibling)
-        dhid_ref[...] = dot(cot_all[r], w_out, CONTRACT_LAST)
+        dhid_ref[...] = dot(cot_all[r], wout_t[...])
         if r > 0:
             arrived(sc_id[r], sc_all.at[r])
         if r == 2:
@@ -230,7 +230,7 @@
             hid[r, at, :] = (pre * phi).astype(BF16)
             dpre[r, at, :] = (dhid_ref[at, :] * slope).astype(BF16)
 
-        back = dot(dpre[r], w_in, CONTRACT_LAST)
+        back = dot(dpre[r], win_t[...])
         if r == 0:
             own_ds[...] = back
         elif r == 2:
@@ -239,13 +239,15 @@
             slot = r // 2
             ds_s[slot] = back.astype(BF16)
             ds_id[r] = send(ds_s.at[slot], ds_r.at[slot], sibling)
+        own_cells = slice(r * cells, r * cells + cells)
+        hid_t[:, own_cells] = hid[r].T
+        if r < 3:
+            sc_t[:, own_cells] = sc_all[r].T
 
     def term_start(h):
-        lhs, rhs = ((hid, cot_all), (sc_all, dpre))[h // 2]
+        lhs, rhs = ((hid_t, cot_all), (sc_t, dpre))[h // 2]
         lanes = slice((h % 2) * 2 * half, (h % 2) * 2 * half + 2 * half)
-        total = dot(lhs[0], rhs[0, :, lanes], CONTRACT_FIRST)
-        for r in range(1, 4):
-            total = total + dot(lhs[r], rhs[r, :, lanes], CONTRACT_FIRST)
+        total = dot(lhs[...], rhs[:, :, lanes].reshape(4 * cells, 2 * half))
         for side in range(2):
             gf[h, side] = total[:, side * half : (side + 1) * half]
             gs[h, side] = total[:, side * half : (side + 1) * half].astype(BF16)
@@ -293,8 +295,10 @@
     ds_s[2] = (keep_ds[...] + ds_r[1].astype(F32)).astype(BF16)
     ds_id[2] = send(ds_s.at[2], ds_r.at[2], across)
 
-    for h in (1, 2, 3):
-        x_ids[h] = term_start(h)
+    x_ids[1] = term_start(1)
+    sc_t[:, 3 * cells :] = sc_all[3].T
+    x_ids[2] = term_start(2)
+    x_ids[3] = term_start(3)
 
     br_id = [None] * 4
     for r in (3, 1, 2, 0):
@@ -455,15 +459,18 @@
 
 
 def write_out(*refs):
-    count = len(refs) // 2
-    sems = refs[-1]
-    copies = [
-        pltpu.make_async_copy(refs[i], refs[count + i], sems.at[i]) for i in range(count)
-    ]
-    for copy in copies:
-        copy.start()
-    for copy in copies:
-        copy.wait()
+    count = (len(refs) - 2) // 3
+    sources, targets, held = (refs[i * count : i * count + count] for i in range(3))
+    in_sems, out_sems = refs[-2:]
+    loads = [pltpu.make_async_copy(sources[i], held[i], in_sems.at[i]) for i in range(count)]
+    stores = [pltpu.make_async_copy(held[i], targets[i], out_sems.at[i]) for i in range(count)]
+    for load in loads:
+        load.start()
+    for load, save in zip(loads, stores):
+        load.wait()
+        save.start()
+    for save in stores:
+        save.wait()
 
 
 def body(tiles, shards, fields, seam_shift, kernel, gain, w_in, w_out, cotangent):
@@ -512,6 +519,10 @@
             vmem(rows, F32),
             vmem((4, cells, hidden), BF16),
             vmem((4, cells, hidden), BF16),
+            vmem((hidden, 4 * cells), BF16),
+            vmem((channels, 4 * cells), BF16),
+            vmem((hidden, channels), BF16),
+            vmem((channels, hidden), BF16),
             vmem((cells, hidden), F32),
             vmem((cells, hidden), F32),
             vmem((2, 3 * height, channels), BF16),
@@ -569,7 +580,8 @@
         out_shape=[jax.ShapeDtypeStruct(out.shape, out.dtype) for out in outs],
         in_specs=[away] * 6,
         out_specs=[away] * 6,
-        scratch_shapes=[pltpu.SemaphoreType.DMA((6,))],
+        scratch_shapes=[pltpu.VMEM(out.shape, out.dtype) for out in outs]
+        + [pltpu.SemaphoreType.DMA((6,)), pltpu.SemaphoreType.DMA((6,))],
         compiler_params=pltpu.CompilerParams(vmem_limit_bytes=58 * 1024 * 1024),
         name="write_out",
     )(*outs)

time: 151 us -> 70 us (0.46)
  Pallas kernels: 150 us -> 69.2 us
    pallas_call x1, Pallas kernels: 84.1 us -> 2.85 us  [body(): pl.pallas_call(write_out, out_shape=[jax.ShapeDtypeStruct(out.shape, out....]
where the time goes in v3:
time: 70 us; the launch traced here: 69.8 us
  Pallas kernels  69.2 us (99%)
    pallas_call x1, Pallas kernels, body(): pl.pallas_call(functools.partial(kernel_body, tiles, hi, height, width, c...  66.3 us
    pallas_call x1, Pallas kernels, body(): pl.pallas_call(write_out, out_shape=[jax.ShapeDtypeStruct(out.shape, out....  2.85 us

profile of v3, /device:TPU:0, one launch (start us, length us, event | category | flops | bytes accessed | tf_op | source)
XLA Modules:
  0.0 69.8 jit_solution(5574358547507829831)
XLA Ops:
  0.6 66.3 %block.1 = (bf16[256,512]{1,0:T(8,128)(2,1)}, bf16[256,512]{1,0:T(8,128)(2,1)}, f32[49,512]{1,0:T(8,128)}, f32[1,512]{1,0:T(1,128)}, f32[512,512]{1,0:T(8,128)}, /*index=5*/f32[512,512]{1,0:T(8,128)}) custom-call(bf16[256,512]{1,0:T(8,128)(2,1)} %bitcast.6, s32[1,2]{1,0:T(1,128)} %seam_ref.1, f32[49,512]{1,0:T(8,128)} %kern_hbm.1, f32[1,512]{1,0:T(1,128)} %bitcast.8, ...), custom_call_target="tpu_custom_call" | custom-call | tf_op jit(solution)/shard_map/block/pallas_call | solution.py:494
  67.0 2.9 %write_out.1 = (bf16[256,512]{1,0:T(8,128)(2,1)}, bf16[256,512]{1,0:T(8,128)(2,1)}, f32[49,512]{1,0:T(8,128)}, f32[1,512]{1,0:T(1,128)}, f32[512,512]{1,0:T(8,128)}, /*index=5*/f32[512,512]{1,0:T(8,128)}) custom-call(bf16[256,512]{1,0:T(8,128)(2,1)} %get-tuple-element.18.refs_0_, bf16[256,512]{1,0:T(8,128)(2,1)} %get-tuple-element.19.refs_1_, ...), custom_call_target="tpu_custom_call" | custom-call | tf_op jit(solution)/shard_map/write_out/pallas_call | solution.py:578

commit v4 on v3

--- a/solution.py
+++ b/solution.py
@@ -53,6 +53,7 @@
 
     cells = height * width
     half = channels // 4
+    piece = channels // hi
     t = lax.axis_index("tile")
     f = lax.axis_index("fsdp")
     west = lax.rem(t + tiles - 1, tiles)
@@ -185,43 +186,87 @@
     loads[3].wait()
     gain = gain_ref[...]
 
-    @pl.loop(0, width)
-    def _(j):
-        at = pl.ds(pl.multiple_of(j * height, height), height)
-        rows = tmp[at, :]
-        centered = rows - jnp.mean(rows, axis=-1, keepdims=True)
-        rstd = lax.rsqrt(jnp.mean(centered * centered, axis=-1, keepdims=True) + eps)
-        unit = centered * rstd
-        normed[at, :] = unit
-        rstd_ref[at, :] = jnp.broadcast_to(rstd, (height, 128))
-        sc_all[0, at, :] = (unit * gain).astype(BF16)
-
-    sc_id = [
-        None,
-        send(sc_all.at[0], sc_all.at[1], sibling),
-        send(sc_all.at[0], sc_all.at[2], across),
-        None,
-    ]
+    sibling_sc, across_sc = [None] * 2, [None] * 2
+    part_rows = [pl.ds(p * (cells // 2), cells // 2) for p in range(2)]
+    for p in range(2):
+
+        @pl.loop(p * (width // 2), (p + 1) * (width // 2))
+        def _(j):
+            at = pl.ds(pl.multiple_of(j * height, height), height)
+            rows = tmp[at, :]
+            centered = rows - jnp.mean(rows, axis=-1, keepdims=True)
+            rstd = lax.rsqrt(jnp.mean(centered * centered, axis=-1, keepdims=True) + eps)
+            unit = centered * rstd
+            normed[at, :] = unit
+            rstd_ref[at, :] = jnp.broadcast_to(rstd, (height, 128))
+            sc_all[0, at, :] = (unit * gain).astype(BF16)
+
+        across_sc[p] = send(sc_all.at[0, part_rows[p]], sc_all.at[2, part_rows[p]], across)
+    sibling_sc = send(sc_all.at[0], sc_all.at[1], sibling)
+    forward_sc = [None] * 2
     loads[4].wait()
     loads[5].wait()
     w_in = win_ref[...]
     w_out = wout_ref[...]
     wout_t[...] = w_out.T
     win_t[...] = w_in.T
+    def term_start(h):
+        lhs, rhs = ((hid_t, cot_all), (sc_t, dpre))[h // 2]
+        lanes = slice((h % 2) * 2 * half, (h % 2) * 2 * half + 2 * half)
+        total = dot(lhs[...], rhs[:, :, lanes].reshape(4 * cells, 2 * half))
+        for side in range(2):
+            gf[h, side] = total[:, side * half : (side + 1) * half]
+            gs[h, side] = total[:, side * half : (side + 1) * half].astype(BF16)
+        return send(gs.at[h, 1 - x], xr.at[h], {"tile": x_peer})
+
+    def term_mid(h, index):
+        arrived(index, xr.at[h])
+        part[h] = gf[h, x] + xr[h].astype(F32)
+        for r in range(1, hi):
+            zs[h, r] = part[h, pl.ds(pl.multiple_of(z_at[r] * piece, piece), piece), :].astype(BF16)
+        return [None] + [
+            send(zs.at[h, r], zr.at[h, r], {"tile": z_peer[r]}) for r in range(1, hi)
+        ]
+
+    def term_sum(h, ids):
+        total = part[h, pl.ds(pl.multiple_of(z * piece, piece), piece), :]
+        for r in range(1, hi):
+            arrived(ids[r], zr.at[h, r])
+            total = total + zr[h, r].astype(F32)
+        agz[h, z] = (total * factor).astype(BF16)
+        ids = [None] + [
+            send(agz.at[h, z], agz.at[h, z], {"tile": z_peer[r]}) for r in range(1, hi)
+        ]
+        last[h] = [send(agz.at[h, z], agx.at[h, z], {"tile": x_peer})]
+        return ids
+
+    def term_put(h, side, value):
+        ref, target = ((woutg_ref, woutg_hbm), (wing_ref, wing_hbm))[h // 2]
+        lanes = pl.ds(pl.multiple_of(((h % 2) * 2 + side) * half, half), half)
+        ref[:, lanes] = value.astype(F32).reshape(channels, half)
+        store(ref.at[:, lanes], target.at[:, lanes])
+
+    def term_spread(h, ids):
+        for r in range(1, hi):
+            arrived(ids[r], agz.at[h, z_from[r]])
+            last[h].append(
+                send(agz.at[h, z_from[r]], agx.at[h, z_from[r]], {"tile": x_peer})
+            )
+        term_put(h, x, agz[h])
+
+    def term_end(h):
+        for r in range(hi):
+            arrived(last[h][r], agx.at[h, z_from[r]])
+        term_put(h, 1 - x, agx[h])
+
     ds_id = [None] * 4
-    for r in range(4):
-        if r > 0:
-            arrived(cot_id[r], cot_all.at[r])
-        if r == 2:
-            cot_id[3] = send(cot_all.at[2], cot_all.at[3], sibling)
-        dhid_ref[...] = dot(cot_all[r], wout_t[...])
-        if r > 0:
-            arrived(sc_id[r], sc_all.at[r])
-        if r == 2:
-            sc_id[3] = send(sc_all.at[2], sc_all.at[3], sibling)
-        pre_ref[...] = dot(sc_all[r], w_in)
-
-        @pl.loop(0, width)
+    x_ids, z_ids, g_ids, last = [None] * 4, [None] * 4, [None] * 4, [None] * 4
+
+    def units(r, p):
+        rows = part_rows[p]
+        pre_ref[rows, :] = dot(sc_all[r, rows, :], w_in)
+
+        @pl.loop(p * (width // 2), (p + 1) * (width // 2))
         def _(j):
             at = pl.ds(pl.multiple_of(j * height, height), height)
             pre = pre_ref[at, :]
@@ -230,6 +275,28 @@
             hid[r, at, :] = (pre * phi).astype(BF16)
             dpre[r, at, :] = (dhid_ref[at, :] * slope).astype(BF16)
 
+        own_cells = slice(r * cells + p * (cells // 2), r * cells + (p + 1) * (cells // 2))
+        hid_t[:, own_cells] = hid[r, rows, :].T
+        if r < 3:
+            sc_t[:, own_cells] = sc_all[r, rows, :].T
+
+    for r in range(4):
+        if r > 0:
+            arrived(cot_id[r], cot_all.at[r])
+        if r == 2:
+            cot_id[3] = send(cot_all.at[2], cot_all.at[3], sibling)
+        dhid_ref[...] = dot(cot_all[r], wout_t[...])
+        if r == 1:
+            arrived(sibling_sc, sc_all.at[1])
+        for p in range(2):
+            if r == 2:
+                arrived(across_sc[p], sc_all.at[2, part_rows[p]])
+                forward_sc[p] = send(sc_all.at[2, part_rows[p]], sc_all.at[3, part_rows[p]], sibling)
+            if r == 3:
+                arrived(forward_sc[p], sc_all.at[3, part_rows[p]])
+            units(r, p)
+        if r == 3:
+            x_ids[0] = term_start(0)
         back = dot(dpre[r], win_t[...])
         if r == 0:
             own_ds[...] = back
@@ -239,69 +306,17 @@
             slot = r // 2
             ds_s[slot] = back.astype(BF16)
             ds_id[r] = send(ds_s.at[slot], ds_r.at[slot], sibling)
-        own_cells = slice(r * cells, r * cells + cells)
-        hid_t[:, own_cells] = hid[r].T
-        if r < 3:
-            sc_t[:, own_cells] = sc_all[r].T
-
-    def term_start(h):
-        lhs, rhs = ((hid_t, cot_all), (sc_t, dpre))[h // 2]
-        lanes = slice((h % 2) * 2 * half, (h % 2) * 2 * half + 2 * half)
-        total = dot(lhs[...], rhs[:, :, lanes].reshape(4 * cells, 2 * half))
-        for side in range(2):
-            gf[h, side] = total[:, side * half : (side + 1) * half]
-            gs[h, side] = total[:, side * half : (side + 1) * half].astype(BF16)
-        return send(gs.at[h, 1 - x], xr.at[h], {"tile": x_peer})
-
-    piece = channels // hi
-
-    def term_mid(h, index):
-        arrived(index, xr.at[h])
-        part[h] = gf[h, x] + xr[h].astype(F32)
-        for r in range(1, hi):
-            zs[h, r] = part[h, pl.ds(pl.multiple_of(z_at[r] * piece, piece), piece), :].astype(BF16)
-        return [None] + [
-            send(zs.at[h, r], zr.at[h, r], {"tile": z_peer[r]}) for r in range(1, hi)
-        ]
-
-    def term_sum(h, ids):
-        total = part[h, pl.ds(pl.multiple_of(z * piece, piece), piece), :]
-        for r in range(1, hi):
-            arrived(ids[r], zr.at[h, r])
-            total = total + zr[h, r].astype(F32)
-        agz[h, z] = (total * factor).astype(BF16)
-        return [None] + [
-            send(agz.at[h, z], agz.at[h, z], {"tile": z_peer[r]}) for r in range(1, hi)
-        ]
-
-    def term_spread(h, ids):
-        for r in range(1, hi):
-            arrived(ids[r], agz.at[h, z_from[r]])
-        return send(agz.at[h], agx.at[h], {"tile": x_peer})
-
-    def term_put(h, side, value):
-        ref = (woutg_ref, wing_ref)[h // 2]
-        lanes = pl.ds(pl.multiple_of(((h % 2) * 2 + side) * half, half), half)
-        ref[:, lanes] = value.astype(F32).reshape(channels, half)
-
-    def term_end(h, index):
-        arrived(index, agx.at[h])
-        term_put(h, 1 - x, agx[h])
-
-    x_ids, z_ids, g_ids, last = [None] * 4, [None] * 4, [None] * 4, [None] * 4
-    x_ids[0] = term_start(0)
-
+
+    x_ids[1] = term_start(1)
     arrived(ds_id[3], ds_r.at[1])
     ds_s[2] = (keep_ds[...] + ds_r[1].astype(F32)).astype(BF16)
     ds_id[2] = send(ds_s.at[2], ds_r.at[2], across)
-
-    x_ids[1] = term_start(1)
     sc_t[:, 3 * cells :] = sc_all[3].T
     x_ids[2] = term_start(2)
     x_ids[3] = term_start(3)
 
     br_id = [None] * 4
-    for r in (3, 1, 2, 0):
+    for r in (3, 2, 1, 0):
         branch = dot(hid[r], w_out)
         if r == 0:
             own_br[...] = branch
@@ -313,7 +328,11 @@
             br_id[r] = send(br_s.at[slot], br_r.at[slot], sibling)
 
     z_ids[0] = term_mid(0, x_ids[0])
+    arrived(br_id[3], br_r.at[1])
+    br_s[2] = (keep_br[...] + br_r[1].astype(F32)).astype(BF16)
+    br_id[2] = send(br_s.at[2], br_r.at[2], across)
     z_ids[1] = term_mid(1, x_ids[1])
+    g_ids[0] = term_sum(0, z_ids[0])
     arrived(ds_id[1], ds_r.at[0])
     arrived(ds_id[2], ds_r.at[2])
 
@@ -360,28 +379,32 @@
 
     kfull[3] = jnp.zeros((16, channels), F32)
     kfull[3, 1:2, :] = jnp.sum(term_gain, axis=0, keepdims=True)
-
-    @pl.loop(0, channels // 128)
-    def _(g):
-        lanes = lanes_of(g)
-        d_here = dpad[:, TOP : TOP + height, lanes]
-        for a in range(7):
-            shifted = ext[:, TOP - 3 + a : TOP - 3 + a + height, lanes]
-            for b in range(7):
-                tap = 7 * a + b
-                both = (d_here * shifted[b : b + width]).reshape(cells // 8, 8, 128)
-                column = jnp.sum(jnp.sum(both, axis=0), axis=0, keepdims=True)
-                kfull[tap // 16, tap % 16 : tap % 16 + 1, lanes] = column
-
+    g_ids[1] = term_sum(1, z_ids[1])
+
+    def tap_sums(first_group, last_group):
+        @pl.loop(first_group, last_group)
+        def _(g):
+            lanes = lanes_of(g)
+            d_here = dpad[:, TOP : TOP + height, lanes]
+            for a in range(7):
+                shifted = ext[:, TOP - 3 + a : TOP - 3 + a + height, lanes]
+                for b in range(7):
+                    tap = 7 * a + b
+                    both = (d_here * shifted[b : b + width]).reshape(cells // 8, 8, 128)
+                    column = jnp.sum(jnp.sum(both, axis=0), axis=0, keepdims=True)
+                    kfull[tap // 16, tap % 16 : tap % 16 + 1, lanes] = column
+
+    tap_sums(0, channels // 256)
+    term_spread(0, g_ids[0])
+    g_ids[2] = term_sum(2, z_ids[2])
+    tap_sums(channels // 256, channels // 128)
     kr_id = [None] + [
         send(kfull.at[f_peer[r]], kr.at[r - 1], {"fsdp": f_peer[r]}) for r in (1, 2, 3)
     ]
-    g_ids[0] = term_sum(0, z_ids[0])
-    g_ids[1] = term_sum(1, z_ids[1])
-
-    arrived(br_id[3], br_r.at[1])
-    br_s[2] = (keep_br[...] + br_r[1].astype(F32)).astype(BF16)
-    br_id[2] = send(br_s.at[2], br_r.at[2], across)
+    g_ids[3] = term_sum(3, z_ids[3])
+    term_spread(1, g_ids[1])
+
+    adjoint(list(range(3, width + 3)))
 
     total = kfull[f]
     for r in (1, 2, 3):
@@ -389,16 +412,12 @@
         total = total + kr[r - 1]
     kl[...] = total
     kl_id = send(kl, klr, {"tile": x_peer})
-    g_ids[2] = term_sum(2, z_ids[2])
-
-    adjoint(list(range(3, width + 3)))
-
+    term_spread(2, g_ids[2])
+    term_end(0)
     arrived(kl_id, klr)
     kz[z] = kl[...] + klr[...]
     kz_id = [None] + [send(kz.at[z], kz.at[z], {"tile": z_peer[r]}) for r in range(1, hi)]
-    g_ids[3] = term_sum(3, z_ids[3])
-    last[0] = term_spread(0, g_ids[0])
-    last[1] = term_spread(1, g_ids[1])
+    term_spread(3, g_ids[3])
 
     arrived(adj_w, adj_r.at[1])
     arrived(adj_e, adj_r.at[0])
@@ -420,8 +439,7 @@
     kf[f] = total * factor
     kf_id = [None] + [send(kf.at[f], kf.at[f], {"fsdp": f_peer[r]}) for r in (1, 2, 3)]
 
-    last[2] = term_spread(2, g_ids[2])
-
+    term_end(1)
     arrived(br_id[1], br_r.at[0])
     arrived(br_id[2], br_r.at[2])
     for j in range(width):
@@ -433,8 +451,7 @@
     gather_lanes(flip2, mixed_ref)
     store(mixed_ref, mixed_hbm)
 
-    last[3] = term_spread(3, g_ids[3])
-
+    term_end(2)
     for r in (1, 2, 3):
         arrived(kf_id[r], kf.at[f_peer[r]])
     for at in range(3):
@@ -444,13 +461,7 @@
     store(kgrad_ref, kgrad_hbm)
     store(ggrad_ref, ggrad_hbm)
 
-    for h in range(4):
-        term_put(h, x, agz[h])
-    for h in range(4):
-        term_end(h, last[h])
-        if h == 1:
-            store(woutg_ref, woutg_hbm)
-    store(wing_ref, wing_hbm)
+    term_end(3)
     for copy in stores:
         copy.wait()
     for copy in started:
@@ -483,7 +494,7 @@
     factor = 1.0 / math.sqrt(cells * tiles * shards)
     half = channels // 4
     piece = channels // hi
-    n_sems = 32 + 4 * (2 + 2 * (hi - 1)) + hi
+    n_sems = 32 + 4 * (1 + 2 * (hi - 1) + hi) + hi
     padded = height + 16
 
     def vmem(shape, kind):
@@ -563,7 +574,7 @@
             vmem(w_in.shape, F32),
             vmem(w_out.shape, F32),
             pltpu.SemaphoreType.DMA((6,)),
-            pltpu.SemaphoreType.DMA((6,)),
+            pltpu.SemaphoreType.DMA((12,)),
             pltpu.SemaphoreType.DMA((n_sems,)),
             pltpu.SemaphoreType.DMA((n_sems,)),
         ],

time: 70 us -> 70.6 us (level)
  no operation moved by 1% of the time
where the time goes in v4:
time: 70.6 us; the launch traced here: 70.2 us
  Pallas kernels  69.5 us (98%)
    pallas_call x1, Pallas kernels, body(): pl.pallas_call(functools.partial(kernel_body, tiles, hi, height, width, c...  66.7 us
    pallas_call x1, Pallas kernels, body(): pl.pallas_call(write_out, out_shape=[jax.ShapeDtypeStruct(out.shape, out....  2.85 us

profile of v4, /device:TPU:0, one launch (start us, length us, event | category | flops | bytes accessed | tf_op | source)
XLA Modules:
  0.0 70.2 jit_solution(16542638789821594808)
XLA Ops:
  0.6 66.7 %block.1 = (bf16[256,512]{1,0:T(8,128)(2,1)}, bf16[256,512]{1,0:T(8,128)(2,1)}, f32[49,512]{1,0:T(8,128)}, f32[1,512]{1,0:T(1,128)}, f32[512,512]{1,0:T(8,128)}, /*index=5*/f32[512,512]{1,0:T(8,128)}) custom-call(bf16[256,512]{1,0:T(8,128)(2,1)} %bitcast.6, s32[1,2]{1,0:T(1,128)} %seam_ref.1, f32[49,512]{1,0:T(8,128)} %kern_hbm.1, f32[1,512]{1,0:T(1,128)} %bitcast.8, ...), custom_call_target="tpu_custom_call" | custom-call | tf_op jit(solution)/shard_map/block/pallas_call | solution.py:505
  67.3 2.9 %write_out.1 = (bf16[256,512]{1,0:T(8,128)(2,1)}, bf16[256,512]{1,0:T(8,128)(2,1)}, f32[49,512]{1,0:T(8,128)}, f32[1,512]{1,0:T(1,128)}, f32[512,512]{1,0:T(8,128)}, /*index=5*/f32[512,512]{1,0:T(8,128)}) custom-call(bf16[256,512]{1,0:T(8,128)(2,1)} %get-tuple-element.18.refs_0_, bf16[256,512]{1,0:T(8,128)(2,1)} %get-tuple-element.19.refs_1_, ...), custom_call_target="tpu_custom_call" | custom-call | tf_op jit(solution)/shard_map/write_out/pallas_call | solution.py:589

commit v5 on v4

--- a/solution.py
+++ b/solution.py
@@ -26,14 +26,14 @@
 def kernel_body(
     tiles, hi, height, width, channels, factor, n_sems,
     x_hbm, seam_ref, kern_hbm, gain_hbm, win_hbm, wout_hbm, cot_hbm,
-    mixed_hbm, fgrad_hbm, kgrad_hbm, ggrad_hbm, wing_hbm, woutg_hbm,
-    ext, dpad, flip, flip2, tmp, normed, rstd_ref, own_ds, keep_ds, own_br, keep_br, hid, dpre, hid_t, sc_t, win_t, wout_t, pre_ref, dhid_ref,
+    mixed_hbm, fgrad_hbm, kgrad_hbm, ggrad_hbm, wg_hbm,
+    ext, dpad, flip, flip2, tmp, normed, rstd_ref, own_ds, keep_ds, own_br, keep_br, hid, dpre, slopes, hid_t, sc_t, win_t, wout_t, pre_ref, dhid_ref,
     hs, hr, adj_s, adj_r, core,
     sc_all, cot_all, ds_s, ds_r, br_s, br_r,
     gf, gs, xr, part, zs, zr, agz, agx,
     kfull, kr, kl, klr, kz, kf,
     x_ref, kern_ref, gain_ref, win_ref, wout_ref, cot_ref,
-    mixed_ref, fgrad_ref, kgrad_ref, ggrad_ref, wing_ref, woutg_ref,
+    mixed_ref, fgrad_ref, kgrad_ref, ggrad_ref,
     load_sems, store_sems, send_sems, recv_sems,
 ):
     pairs = (
@@ -158,37 +158,35 @@
         @pl.loop(0, channels // 128)
         def _(g):
             lanes = lanes_of(g)
-            total = [
-                jnp.zeros((height, 128), F32) if fresh else tmp[rows_of(j), lanes]
-                for j in range(width)
-            ]
+            reached = [j for j in range(width) if any(j <= c <= j + 6 for c in columns)]
+            total = {
+                j: jnp.zeros((height, 128), F32) if fresh else tmp[rows_of(j), lanes]
+                for j in reached
+            }
             for a in range(7):
                 first = TOP - 3 + a
                 shifted = {c: ext[c, first : first + height, lanes] for c in columns}
                 for b in range(7):
                     tap = kern_ref[pl.ds(7 * a + b, 1), lanes]
-                    for j in range(width):
+                    for j in reached:
                         if j + b in shifted:
                             total[j] = total[j] + shifted[j + b] * tap
-            for j in range(width):
+            for j in reached:
                 tmp[rows_of(j), lanes] = total[j]
 
     loads[2].wait()
     conv_part(list(range(3, width + 3)), True)
-    arrived(halo_w, hr.at[1])
-    arrived(halo_e, hr.at[0])
+    loads[3].wait()
+    gain = gain_ref[...]
+    sibling_sc, across_sc = [None] * 2, [None] * 2
+    part_rows = [pl.ds(p * (cells // 2), cells // 2) for p in range(2)]
     for side, first in ((0, 0), (1, width + 3)):
+        p = side
+        arrived((halo_e, halo_w)[side], hr.at[side])
         pick = picker(seam_ref[0, side])
         for j in range(3):
             ext[first + j, TOP : TOP + height, :] = dot(pick, hr[side, rows_of(j), :])
-    conv_part([0, 1, 2, width + 3, width + 4, width + 5], False)
-
-    loads[3].wait()
-    gain = gain_ref[...]
-
-    sibling_sc, across_sc = [None] * 2, [None] * 2
-    part_rows = [pl.ds(p * (cells // 2), cells // 2) for p in range(2)]
-    for p in range(2):
+        conv_part([first, first + 1, first + 2], False)
 
         @pl.loop(p * (width // 2), (p + 1) * (width // 2))
         def _(j):
@@ -240,24 +238,18 @@
         last[h] = [send(agz.at[h, z], agx.at[h, z], {"tile": x_peer})]
         return ids
 
-    def term_put(h, side, value):
-        ref, target = ((woutg_ref, woutg_hbm), (wing_ref, wing_hbm))[h // 2]
-        lanes = pl.ds(pl.multiple_of(((h % 2) * 2 + side) * half, half), half)
-        ref[:, lanes] = value.astype(F32).reshape(channels, half)
-        store(ref.at[:, lanes], target.at[:, lanes])
-
     def term_spread(h, ids):
         for r in range(1, hi):
             arrived(ids[r], agz.at[h, z_from[r]])
             last[h].append(
                 send(agz.at[h, z_from[r]], agx.at[h, z_from[r]], {"tile": x_peer})
             )
-        term_put(h, x, agz[h])
+        store(agz.at[h], wg_hbm.at[h, x])
 
     def term_end(h):
         for r in range(hi):
             arrived(last[h][r], agx.at[h, z_from[r]])
-        term_put(h, 1 - x, agx[h])
+        store(agx.at[h], wg_hbm.at[h, 1 - x])
 
     ds_id = [None] * 4
     x_ids, z_ids, g_ids, last = [None] * 4, [None] * 4, [None] * 4, [None] * 4
@@ -271,32 +263,20 @@
             at = pl.ds(pl.multiple_of(j * height, height), height)
             pre = pre_ref[at, :]
             phi = 0.5 * (1.0 + lax.erf(pre * inv_root2))
-            slope = phi + pre * inv_root_tau * jnp.exp(-0.5 * pre * pre)
+            slopes[r % 2, at, :] = phi + pre * inv_root_tau * jnp.exp(-0.5 * pre * pre)
             hid[r, at, :] = (pre * phi).astype(BF16)
-            dpre[r, at, :] = (dhid_ref[at, :] * slope).astype(BF16)
 
         own_cells = slice(r * cells + p * (cells // 2), r * cells + (p + 1) * (cells // 2))
         hid_t[:, own_cells] = hid[r, rows, :].T
-        if r < 3:
-            sc_t[:, own_cells] = sc_all[r, rows, :].T
-
-    for r in range(4):
-        if r > 0:
-            arrived(cot_id[r], cot_all.at[r])
-        if r == 2:
-            cot_id[3] = send(cot_all.at[2], cot_all.at[3], sibling)
+
+    def units_back(r):
         dhid_ref[...] = dot(cot_all[r], wout_t[...])
-        if r == 1:
-            arrived(sibling_sc, sc_all.at[1])
-        for p in range(2):
-            if r == 2:
-                arrived(across_sc[p], sc_all.at[2, part_rows[p]])
-                forward_sc[p] = send(sc_all.at[2, part_rows[p]], sc_all.at[3, part_rows[p]], sibling)
-            if r == 3:
-                arrived(forward_sc[p], sc_all.at[3, part_rows[p]])
-            units(r, p)
-        if r == 3:
-            x_ids[0] = term_start(0)
+
+        @pl.loop(0, width)
+        def _(j):
+            at = pl.ds(pl.multiple_of(j * height, height), height)
+            dpre[r, at, :] = (dhid_ref[at, :] * slopes[r % 2, at, :]).astype(BF16)
+
         back = dot(dpre[r], win_t[...])
         if r == 0:
             own_ds[...] = back
@@ -307,11 +287,33 @@
             ds_s[slot] = back.astype(BF16)
             ds_id[r] = send(ds_s.at[slot], ds_r.at[slot], sibling)
 
+    for r in (0, 1):
+        if r == 1:
+            arrived(cot_id[1], cot_all.at[1])
+            arrived(sibling_sc, sc_all.at[1])
+        for p in range(2):
+            units(r, p)
+        units_back(r)
+        sc_t[:, r * cells : (r + 1) * cells] = sc_all[r].T
+    arrived(cot_id[2], cot_all.at[2])
+    cot_id[3] = send(cot_all.at[2], cot_all.at[3], sibling)
+    for p in range(2):
+        arrived(across_sc[p], sc_all.at[2, part_rows[p]])
+        forward_sc[p] = send(sc_all.at[2, part_rows[p]], sc_all.at[3, part_rows[p]], sibling)
+        units(2, p)
+    for p in range(2):
+        arrived(forward_sc[p], sc_all.at[3, part_rows[p]])
+        units(3, p)
+    arrived(cot_id[3], cot_all.at[3])
+    x_ids[0] = term_start(0)
+    units_back(3)
     x_ids[1] = term_start(1)
+    units_back(2)
     arrived(ds_id[3], ds_r.at[1])
     ds_s[2] = (keep_ds[...] + ds_r[1].astype(F32)).astype(BF16)
     ds_id[2] = send(ds_s.at[2], ds_r.at[2], across)
-    sc_t[:, 3 * cells :] = sc_all[3].T
+    for r in (2, 3):
+        sc_t[:, r * cells : (r + 1) * cells] = sc_all[r].T
     x_ids[2] = term_start(2)
     x_ids[3] = term_start(3)
 
@@ -368,18 +370,10 @@
             for c in columns:
                 core[c, :, lanes] = total[c]
 
-    adjoint([0, 1, 2, width + 3, width + 4, width + 5])
-    for side, first in ((0, 0), (1, width + 3)):
-        pick = picker(-seam_ref[0, side])
-        for j in range(3):
-            adj_s[side, rows_of(j), :] = dot(pick, core[first + j].astype(BF16)).astype(BF16)
-    adj_w = send(adj_s.at[0], adj_r.at[1], {"tile": west})
-    adj_e = send(adj_s.at[1], adj_r.at[0], {"tile": east})
-    z_ids[3] = term_mid(3, x_ids[3])
-
     kfull[3] = jnp.zeros((16, channels), F32)
     kfull[3, 1:2, :] = jnp.sum(term_gain, axis=0, keepdims=True)
     g_ids[1] = term_sum(1, z_ids[1])
+    z_ids[3] = term_mid(3, x_ids[3])
 
     def tap_sums(first_group, last_group):
         @pl.loop(first_group, last_group)
@@ -401,8 +395,16 @@
     kr_id = [None] + [
         send(kfull.at[f_peer[r]], kr.at[r - 1], {"fsdp": f_peer[r]}) for r in (1, 2, 3)
     ]
+    term_spread(1, g_ids[1])
     g_ids[3] = term_sum(3, z_ids[3])
-    term_spread(1, g_ids[1])
+
+    adjoint([0, 1, 2, width + 3, width + 4, width + 5])
+    for side, first in ((0, 0), (1, width + 3)):
+        pick = picker(-seam_ref[0, side])
+        for j in range(3):
+            adj_s[side, rows_of(j), :] = dot(pick, core[first + j].astype(BF16)).astype(BF16)
+    adj_w = send(adj_s.at[0], adj_r.at[1], {"tile": west})
+    adj_e = send(adj_s.at[1], adj_r.at[0], {"tile": east})
 
     adjoint(list(range(3, width + 3)))
 
@@ -470,18 +472,38 @@
 
 
 def write_out(*refs):
-    count = (len(refs) - 2) // 3
-    sources, targets, held = (refs[i * count : i * count + count] for i in range(3))
-    in_sems, out_sems = refs[-2:]
-    loads = [pltpu.make_async_copy(sources[i], held[i], in_sems.at[i]) for i in range(count)]
-    stores = [pltpu.make_async_copy(held[i], targets[i], out_sems.at[i]) for i in range(count)]
-    for load in loads:
+    sources, targets, held, wide = refs[:5], refs[5:11], refs[11:16], refs[16:18]
+    in_sems, out_sems = refs[18:]
+    order = list(range(4))
+    loads = [pltpu.make_async_copy(sources[i], held[i], in_sems.at[i]) for i in order]
+    terms = [
+        pltpu.make_async_copy(sources[4].at[h], held[4].at[h], in_sems.at[4 + h])
+        for h in range(4)
+    ]
+    for load in terms + loads:
         load.start()
-    for load, save in zip(loads, stores):
-        load.wait()
-        save.start()
-    for save in stores:
-        save.wait()
+    stores = []
+
+    def save(src, dst):
+        stores.append(pltpu.make_async_copy(src, dst, out_sems.at[len(stores)]))
+        stores[-1].start()
+
+    _, sides, hi, piece, half = held[4].shape
+    for h in range(4):
+        terms[h].wait()
+        which = 1 - h // 2
+        for side in range(sides):
+            first = ((h % 2) * 2 + side) * half
+            wide[which][:, first : first + half] = (
+                held[4][h, side].astype(F32).reshape(hi * piece, half)
+            )
+        if h % 2 == 1:
+            save(wide[which], targets[4 + which])
+    for i in order:
+        loads[i].wait()
+        save(held[i], targets[i])
+    for copy in stores:
+        copy.wait()
 
 
 def body(tiles, shards, fields, seam_shift, kernel, gain, w_in, w_out, cotangent):
@@ -509,13 +531,12 @@
             jax.ShapeDtypeStruct(rows, BF16),
             jax.ShapeDtypeStruct(kernel.shape, F32),
             jax.ShapeDtypeStruct((1, channels), F32),
-            jax.ShapeDtypeStruct(w_in.shape, F32),
-            jax.ShapeDtypeStruct(w_out.shape, F32),
+            jax.ShapeDtypeStruct((4, 2, hi, piece, half), BF16),
         ),
         in_specs=[
             away, pl.BlockSpec(memory_space=pltpu.SMEM), away, away, away, away, away,
         ],
-        out_specs=[away] * 6,
+        out_specs=[away] * 5,
         scratch_shapes=[
             vmem((width + 6, padded, channels), F32),
             vmem((width, padded, channels), F32),
@@ -530,6 +551,7 @@
             vmem(rows, F32),
             vmem((4, cells, hidden), BF16),
             vmem((4, cells, hidden), BF16),
+            vmem((2, cells, hidden), F32),
             vmem((hidden, 4 * cells), BF16),
             vmem((channels, 4 * cells), BF16),
             vmem((hidden, channels), BF16),
@@ -571,8 +593,6 @@
             vmem(rows, BF16),
             vmem(kernel.shape, F32),
             vmem((1, channels), F32),
-            vmem(w_in.shape, F32),
-            vmem(w_out.shape, F32),
             pltpu.SemaphoreType.DMA((6,)),
             pltpu.SemaphoreType.DMA((12,)),
             pltpu.SemaphoreType.DMA((n_sems,)),
@@ -588,11 +608,13 @@
     )
     outs = pl.pallas_call(
         write_out,
-        out_shape=[jax.ShapeDtypeStruct(out.shape, out.dtype) for out in outs],
-        in_specs=[away] * 6,
+        out_shape=[jax.ShapeDtypeStruct(out.shape, out.dtype) for out in outs[:4]]
+        + [jax.ShapeDtypeStruct(w.shape, F32) for w in (w_in, w_out)],
+        in_specs=[away] * 5,
         out_specs=[away] * 6,
         scratch_shapes=[pltpu.VMEM(out.shape, out.dtype) for out in outs]
-        + [pltpu.SemaphoreType.DMA((6,)), pltpu.SemaphoreType.DMA((6,))],
+        + [pltpu.VMEM(w.shape, F32) for w in (w_in, w_out)]
+        + [pltpu.SemaphoreType.DMA((8,)), pltpu.SemaphoreType.DMA((6,))],
         compiler_params=pltpu.CompilerParams(vmem_limit_bytes=58 * 1024 * 1024),
         name="write_out",
     )(*outs)

time: 70.6 us -> 70.7 us (level)
  the two profiles are of different devices: /device:TPU:0 before, /device:TPU:7 now
where the time goes in v5:
time: 70.7 us; the launch traced here: 70.5 us
  Pallas kernels  69.9 us (99%)
    pallas_call x1, Pallas kernels, body(): pl.pallas_call(functools.partial(kernel_body, tiles, hi, height, width, c...  67.1 us
    pallas_call x1, Pallas kernels, body(): pl.pallas_call(write_out, out_shape=[jax.ShapeDtypeStruct(out.shape, out....  2.73 us

profile of v5, /device:TPU:7, one launch (start us, length us, event | category | flops | bytes accessed | tf_op | source)
XLA Modules:
  0.0 70.5 jit_solution(18305659552400948064)
XLA Ops:
  0.6 67.1 %block.1 = (bf16[256,512]{1,0:T(8,128)(2,1)}, bf16[256,512]{1,0:T(8,128)(2,1)}, f32[49,512]{1,0:T(8,128)}, f32[1,512]{1,0:T(1,128)}, bf16[4,2,4,128,128]{4,3,2,1,0:T(8,128)(2,1)}) custom-call(bf16[256,512]{1,0:T(8,128)(2,1)} %bitcast.6, s32[1,2]{1,0:T(1,128)} %seam_ref.1, f32[49,512]{1,0:T(8,128)} %kern_hbm.1, f32[1,512]{1,0:T(1,128)} %bitcast.8, ...), custom_call_target="tpu_custom_call" | custom-call | tf_op jit(solution)/shard_map/block/pallas_call | solution.py:527
  67.8 2.7 %write_out.1 = (bf16[256,512]{1,0:T(8,128)(2,1)}, bf16[256,512]{1,0:T(8,128)(2,1)}, f32[49,512]{1,0:T(8,128)}, f32[1,512]{1,0:T(1,128)}, f32[512,512]{1,0:T(8,128)}, /*index=5*/f32[512,512]{1,0:T(8,128)}) custom-call(bf16[256,512]{1,0:T(8,128)(2,1)} %get-tuple-element.17.refs_0_, bf16[256,512]{1,0:T(8,128)(2,1)} %get-tuple-element.18.refs_1_, ...), custom_call_target="tpu_custom_call" | custom-call | tf_op jit(solution)/shard_map/write_out/pallas_call | solution.py:609
